TPU v7x, 32 devices: a whole 2x2x4 slice. The times are simulated.
32 devices in a mesh: rep: 4 (over x, core), ep: 8 (over z, y).
Axes of the slice: x: 2, y: 2, z: 4, core: 2. Of those that a mesh axis runs over, the one named last changes fastest.
Arguments:
- tokens: bfloat16 [8192, 1536], P(('rep', 'ep')), may hold values from -6 to 6
- segments: int32 [32, 256], P(('rep', 'ep')), may hold values from 0 to 7, never falling along the last dimension, each value on 1 to 128 neighbouring positions
- routes: int32 [8192, 4], P(('rep', 'ep')), may hold values from 0 to 7, all different within a row; in each aligned block of 256 rows (0 to 255, 256 to 511, ...) at most 192 rows name the same one
- valid_mask: int32 [32, 256], P(('rep', 'ep')), may hold values from 0 to 1, as said below
- teacher: bfloat16 [8192, 1536], P(('rep', 'ep')), may hold values from -6 to 6
- gain_one: bfloat16 [1536], replicated, may hold values from 0.5 to 1.5
- w_query: bfloat16 [1536, 1536], replicated, may hold values from -0.15625 to 0.15625
- w_key: bfloat16 [1536, 256], replicated, may hold values from -0.15625 to 0.15625
- w_value: bfloat16 [1536, 256], replicated, may hold values from -0.15625 to 0.15625
- w_out: bfloat16 [1536, 1536], replicated, may hold values from -0.4375 to 0.4375
- gain_two: bfloat16 [1536], replicated, may hold values from 0.5 to 1.5
- router: bfloat16 [1536, 8], replicated, may hold values from -0.078125 to 0.078125
- w_gate: bfloat16 [8, 1536, 768], P('ep'), may hold values from -0.15625 to 0.15625
- w_up: bfloat16 [8, 1536, 768], P('ep'), may hold values from -0.15625 to 0.15625
- w_down: bfloat16 [8, 768, 1536], P('ep'), may hold values from -0.4375 to 0.4375
Outputs:
- output: bfloat16 [8192, 1536], P(('rep', 'ep'))
- loss_value: float32 [], replicated
- grad_tokens: float32 [8192, 1536], P(('rep', 'ep'))
- grad_gain_one: float32 [1536], replicated
- grad_w_query: float32 [1536, 1536], P('ep')
- grad_w_key: float32 [1536, 256], P('ep')
- grad_w_value: float32 [1536, 256], P('ep')
- grad_w_out: float32 [1536, 1536], P('ep')
- grad_gain_two: float32 [1536], replicated
- grad_router: float32 [1536, 8], replicated
- grad_w_gate: float32 [8, 1536, 768], P('ep', 'rep')
- grad_w_up: float32 [8, 1536, 768], P('ep', 'rep')
- grad_w_down: float32 [8, 768, 1536], P('ep', 'rep')
Inputs may be any that keep to these rules, and one draw needn't show every extreme that they name: `segments`: segment numbers never fall along a sequence. `routes`: among the 256 rows of one device no expert is named more than 192 times; a token names 4 different experts. `valid_mask`: the first token of every sequence is valid.
All inputs are finite; a program needn't handle non-finite values.
Results may differ from a plain program's by a relative error of at most 0.018.
Values may be sent and summed in bfloat16 or wider, within the bound.
No kernel may reach another device: no remote copies, remote signals or barrier semaphores. Data moves between devices by JAX's collectives and lax.ppermute only.
A program may use at most 192 MiB of HBM per device.

v0:
```python
import jax
import jax.numpy as jnp
from jax import lax
from jax.sharding import PartitionSpec as P

H = 12
KVH = 2
HEAD = 128


EPSILON = 1e-06
ROPE_BASE = 10000.0
NEG_FILL = -1e30


def rms_norm(values, gain):
    inverse = lax.rsqrt(jnp.mean(values * values, axis=-1, keepdims=True) + EPSILON)
    return values * inverse * gain


def rotate(values, direction):
    length = values.shape[-3]
    half_dim = values.shape[-1] // 2
    frequency = ROPE_BASE ** (-jnp.arange(half_dim, dtype=jnp.float32) / half_dim)
    angles = jnp.arange(length, dtype=jnp.float32)[:, None] * frequency[None, :] * direction
    cosine = jnp.cos(angles)[:, None, :]
    sinusoid = jnp.sin(angles)[:, None, :]
    first_half = values[..., :half_dim]
    second_half = values[..., half_dim:]
    return jnp.concatenate(
        [
            first_half * cosine - second_half * sinusoid,
            second_half * cosine + first_half * sinusoid,
        ],
        axis=-1,
    )


def activate(gate_pre, up_pre):
    return jax.nn.gelu(gate_pre, approximate=True) * up_pre


def shards(
    tokens,
    segments,
    routes,
    valid_mask,
    teacher,
    gain_one,
    w_query,
    w_key,
    w_value,
    w_out,
    gain_two,
    router,
    w_gate,
    w_up,
    w_down,
):
    length = tokens.shape[0]
    model_width = tokens.shape[1]
    top_count = routes.shape[1]
    experts_all = router.shape[1]
    experts_dev = w_gate.shape[0]
    group_size = lax.axis_size("ep")
    capacity = 3 * length * top_count // (2 * experts_all)
    tokens_all = length * lax.axis_size("rep") * group_size
    groups = H // KVH
    score_scale = HEAD ** (-0.5)
    valid_rows = valid_mask.reshape(length).astype(jnp.float32)
    count_total = lax.psum(jnp.sum(valid_rows), ("rep", "ep"))
    token_values = tokens.astype(jnp.float32)
    normed_one, norm_one_pull = jax.vjp(rms_norm, token_values, gain_one.astype(jnp.float32))
    normed_low = normed_one.astype(jnp.bfloat16)
    query_pre = jnp.dot(normed_low, w_query, preferred_element_type=jnp.float32).reshape(
        length, H, HEAD
    )
    key_pre = jnp.dot(normed_low, w_key, preferred_element_type=jnp.float32).reshape(
        length, KVH, HEAD
    )
    value_low = (
        jnp.dot(normed_low, w_value, preferred_element_type=jnp.float32)
        .astype(jnp.bfloat16)
        .reshape(length, KVH, HEAD)
    )
    query_rot = rotate(query_pre, 1.0).astype(jnp.bfloat16).reshape(length, KVH, groups, HEAD)
    key_rot = rotate(key_pre, 1.0).astype(jnp.bfloat16)
    places = jnp.arange(length)
    seg_row = segments.reshape(length)
    allowed = (seg_row[:, None] == seg_row[None, :]) & (places[:, None] >= places[None, :])

    def masked_scores():
        raw_scores = jnp.einsum(
            "qkgc,pkc->kgqp", query_rot, key_rot, preferred_element_type=jnp.float32
        )
        return jnp.where(allowed, raw_scores * score_scale, NEG_FILL)

    scores = masked_scores()
    row_peak = jnp.max(scores, axis=-1, keepdims=True)
    exp_terms = jnp.exp(scores - row_peak)
    row_total = jnp.sum(exp_terms, axis=-1, keepdims=True)
    log_total = row_peak + jnp.log(row_total)
    weights_low = (exp_terms / row_total).astype(jnp.bfloat16)
    context = jnp.einsum(
        "kgqp,pkc->qkgc", weights_low, value_low, preferred_element_type=jnp.float32
    )
    context = context.reshape(length, H * HEAD).astype(jnp.bfloat16)
    mixed_rows = token_values + jnp.dot(context, w_out, preferred_element_type=jnp.float32)
    normed_two, norm_two_pull = jax.vjp(rms_norm, mixed_rows, gain_two.astype(jnp.float32))
    moe_in = normed_two.astype(jnp.bfloat16)
    logits = jnp.dot(moe_in, router, preferred_element_type=jnp.float32)
    expert_ids = jnp.arange(experts_all, dtype=jnp.int32)
    route_hot = routes[:, :, None] == expert_ids[None, None, :]
    chosen = jnp.sum(jnp.where(route_hot, logits[:, None, :], 0.0), axis=2)
    chosen_peak = jnp.max(chosen, axis=1, keepdims=True)
    gate_terms = jnp.exp(chosen - chosen_peak)
    gate_weights = gate_terms / jnp.sum(gate_terms, axis=1, keepdims=True)
    pair_count = length * top_count
    flat_hot = route_hot.reshape(pair_count, experts_all).astype(jnp.int32)
    slot_rank = jnp.sum((jnp.cumsum(flat_hot, axis=0) - 1) * flat_hot, axis=1)
    slot_id = routes.reshape(pair_count) * capacity + slot_rank
    slot_pair = (
        jnp.full((experts_all * capacity,), pair_count, jnp.int32)
        .at[slot_id]
        .set(jnp.arange(pair_count, dtype=jnp.int32))
    )
    slot_token = jnp.where(slot_pair < pair_count, slot_pair // top_count, length)
    padded_in = jnp.concatenate([moe_in, jnp.zeros((1, model_width), jnp.bfloat16)], axis=0)
    send_rows = padded_in[slot_token].reshape(group_size, experts_dev, capacity, model_width)
    arrived = lax.all_to_all(send_rows, "ep", split_axis=0, concat_axis=0, tiled=True)
    gate_pre = jnp.einsum("secd,edf->secf", arrived, w_gate, preferred_element_type=jnp.float32)
    up_pre = jnp.einsum("secd,edf->secf", arrived, w_up, preferred_element_type=jnp.float32)
    hidden = activate(gate_pre, up_pre).astype(jnp.bfloat16)
    result = jnp.einsum(
        "secf,efd->secd", hidden, w_down, preferred_element_type=jnp.float32
    ).astype(jnp.bfloat16)
    exchanged = (result, arrived, gate_pre, up_pre)
    expert_out = exchanged[0]
    arrived = exchanged[1]
    returned = lax.all_to_all(expert_out, "ep", split_axis=0, concat_axis=0, tiled=True)
    picked = returned.reshape(experts_all * capacity, model_width)[slot_id].reshape(
        length, top_count, model_width
    )
    moe_out = jnp.einsum("tk,tkd->td", gate_weights, picked, preferred_element_type=jnp.float32)
    output_rows = mixed_rows + moe_out
    residual_gap = output_rows - teacher.astype(jnp.float32)
    numerator = jnp.sum(valid_rows * jnp.sum(residual_gap * residual_gap, axis=-1))
    grad_out = 2.0 * tokens_all / count_total * valid_rows[:, None] * residual_gap
    grad_gates = jnp.einsum("td,tkd->tk", grad_out, picked, preferred_element_type=jnp.float32)
    grad_picked = (
        (gate_weights[:, :, None] * grad_out[:, None, :])
        .astype(jnp.bfloat16)
        .reshape(pair_count, model_width)
    )
    padded_grad = jnp.concatenate([grad_picked, jnp.zeros((1, model_width), jnp.bfloat16)], axis=0)
    send_grad = padded_grad[slot_pair].reshape(group_size, experts_dev, capacity, model_width)
    arrived_grad = lax.all_to_all(send_grad, "ep", split_axis=0, concat_axis=0, tiled=True)
    gate_pre = exchanged[2]
    up_pre = exchanged[3]
    hidden_val, act_pull = jax.vjp(activate, gate_pre, up_pre)
    hidden_low = hidden_val.astype(jnp.bfloat16)
    grad_w_down = jnp.einsum(
        "secf,secd->efd", hidden_low, arrived_grad, preferred_element_type=jnp.float32
    )
    grad_hidden = jnp.einsum(
        "secd,efd->secf", arrived_grad, w_down, preferred_element_type=jnp.float32
    )
    grad_gate_pre, grad_up_pre = act_pull(grad_hidden)
    grad_gate_low = grad_gate_pre.astype(jnp.bfloat16)
    grad_up_low = grad_up_pre.astype(jnp.bfloat16)
    grad_w_gate = jnp.einsum(
        "secd,secf->edf", arrived, grad_gate_low, preferred_element_type=jnp.float32
    )
    grad_w_up = jnp.einsum(
        "secd,secf->edf", arrived, grad_up_low, preferred_element_type=jnp.float32
    )
    grad_rows = (
        jnp.einsum("secf,edf->secd", grad_gate_low, w_gate, preferred_element_type=jnp.float32)
        + jnp.einsum("secf,edf->secd", grad_up_low, w_up, preferred_element_type=jnp.float32)
    ).astype(jnp.bfloat16)
    back_rows = lax.all_to_all(grad_rows, "ep", split_axis=0, concat_axis=0, tiled=True)
    back_picked = back_rows.reshape(experts_all * capacity, model_width)[slot_id].reshape(
        length, top_count, model_width
    )
    grad_moe_in = jnp.sum(back_picked.astype(jnp.float32), axis=1)
    expert_grads = (
        lax.psum_scatter(
            grad_w_gate.astype(jnp.bfloat16), "rep", scatter_dimension=1, tiled=True
        ).astype(jnp.float32),
        lax.psum_scatter(
            grad_w_up.astype(jnp.bfloat16), "rep", scatter_dimension=1, tiled=True
        ).astype(jnp.float32),
        lax.psum_scatter(
            grad_w_down.astype(jnp.bfloat16), "rep", scatter_dimension=1, tiled=True
        ).astype(jnp.float32),
    )
    grad_chosen = gate_weights * (
        grad_gates - jnp.sum(gate_weights * grad_gates, axis=1, keepdims=True)
    )
    grad_logits = jnp.sum(jnp.where(route_hot, grad_chosen[:, :, None], 0.0), axis=1).astype(
        jnp.bfloat16
    )
    grad_router = jnp.einsum("td,te->de", moe_in, grad_logits, preferred_element_type=jnp.float32)
    grad_moe_in = grad_moe_in + jnp.einsum(
        "te,de->td", grad_logits, router, preferred_element_type=jnp.float32
    )
    grad_norm_two, grad_gain_two = norm_two_pull(grad_moe_in)
    grad_mixed = grad_out + grad_norm_two
    grad_branch = grad_mixed.astype(jnp.bfloat16)
    grad_w_out = jnp.einsum("te,td->ed", context, grad_branch, preferred_element_type=jnp.float32)
    grad_context = jnp.einsum("td,ed->te", grad_branch, w_out, preferred_element_type=jnp.float32)
    grad_context = grad_context.astype(jnp.bfloat16).reshape(length, KVH, groups, HEAD)
    attn_weights = jnp.exp(masked_scores() - log_total)
    grad_weights = jnp.einsum(
        "qkgc,pkc->kgqp", grad_context, value_low, preferred_element_type=jnp.float32
    )
    row_term = jnp.sum(attn_weights * grad_weights, axis=-1, keepdims=True)
    grad_scores = (attn_weights * (grad_weights - row_term)).astype(jnp.bfloat16)
    grad_query_rot = (
        jnp.einsum("kgqp,pkc->qkgc", grad_scores, key_rot, preferred_element_type=jnp.float32)
        * score_scale
    )
    grad_key_rot = (
        jnp.einsum("kgqp,qkgc->pkc", grad_scores, query_rot, preferred_element_type=jnp.float32)
        * score_scale
    )
    grad_value = jnp.einsum(
        "kgqp,qkgc->pkc",
        attn_weights.astype(jnp.bfloat16),
        grad_context,
        preferred_element_type=jnp.float32,
    )
    grad_value = grad_value.astype(jnp.bfloat16).reshape(length, KVH * HEAD)
    grad_query = (
        rotate(grad_query_rot.reshape(length, H, HEAD), -1.0)
        .astype(jnp.bfloat16)
        .reshape(length, H * HEAD)
    )
    grad_key = rotate(grad_key_rot, -1.0).astype(jnp.bfloat16).reshape(length, KVH * HEAD)
    grad_w_query = jnp.einsum(
        "td,te->de", normed_low, grad_query, preferred_element_type=jnp.float32
    )
    grad_w_key = jnp.einsum("td,te->de", normed_low, grad_key, preferred_element_type=jnp.float32)
    grad_w_value = jnp.einsum(
        "td,te->de", normed_low, grad_value, preferred_element_type=jnp.float32
    )
    grad_normed = (
        jnp.einsum("te,de->td", grad_query, w_query, preferred_element_type=jnp.float32)
        + jnp.einsum("te,de->td", grad_key, w_key, preferred_element_type=jnp.float32)
        + jnp.einsum("te,de->td", grad_value, w_value, preferred_element_type=jnp.float32)
    )
    grad_norm_one, grad_gain_one = norm_one_pull(grad_normed)
    grad_tokens = grad_mixed + grad_norm_one
    attn_grads = (grad_w_query, grad_w_key, grad_w_value, grad_w_out)
    partial_rows = (
        lax.psum_scatter(
            attn_grads[0].astype(jnp.bfloat16), "ep", scatter_dimension=0, tiled=True
        ).astype(jnp.float32),
        lax.psum_scatter(
            attn_grads[1].astype(jnp.bfloat16), "ep", scatter_dimension=0, tiled=True
        ).astype(jnp.float32),
        lax.psum_scatter(
            attn_grads[2].astype(jnp.bfloat16), "ep", scatter_dimension=0, tiled=True
        ).astype(jnp.float32),
        lax.psum_scatter(
            attn_grads[3].astype(jnp.bfloat16), "ep", scatter_dimension=0, tiled=True
        ).astype(jnp.float32),
    )
    shares = (
        lax.psum(partial_rows[0].astype(jnp.bfloat16), "rep").astype(jnp.float32),
        lax.psum(partial_rows[1].astype(jnp.bfloat16), "rep").astype(jnp.float32),
        lax.psum(partial_rows[2].astype(jnp.bfloat16), "rep").astype(jnp.float32),
        lax.psum(partial_rows[3].astype(jnp.bfloat16), "rep").astype(jnp.float32),
    )
    small_sums = lax.psum((grad_router, grad_gain_one, grad_gain_two, numerator), ("rep", "ep"))
    loss_value = small_sums[3] / count_total
    return (
        output_rows.astype(jnp.bfloat16),
        loss_value,
        grad_tokens,
        small_sums[1],
        shares[0],
        shares[1],
        shares[2],
        shares[3],
        small_sums[2],
        small_sums[0],
        expert_grads[0],
        expert_grads[1],
        expert_grads[2],
    )


def solution(mesh):
    placed = (
        P(("rep", "ep"), None),
        P(("rep", "ep"), None),
        P(("rep", "ep"), None),
        P(("rep", "ep"), None),
        P(("rep", "ep"), None),
        P(),
        P(),
        P(),
        P(),
        P(),
        P(),
        P(),
        P("ep", None, None),
        P("ep", None, None),
        P("ep", None, None),
    )
    return jax.shard_map(
        shards,
        mesh=mesh,
        in_specs=placed,
        out_specs=(
            P(("rep", "ep"), None),
            P(),
            P(("rep", "ep"), None),
            P(),
            P("ep", None),
            P("ep", None),
            P("ep", None),
            P("ep", None),
            P(),
            P(),
            P("ep", "rep", None),
            P("ep", "rep", None),
            P("ep", "rep", None),
        ),
        check_vma=False,
    )
```

profile of v0, /device:TPU:0, one launch (start us, length us, event | category | flops | bytes accessed | tf_op | source)
XLA Modules:
  0.0 1037.5 jit_solution(6621237418448082256)
XLA Ops:
  50.1 6.3 gather_fusion
  56.3 112.0 %all_to_all.20 = bf16[8,1,192,1536]{3,2,1,0:T(8,128)(2,1)S(1)} all-to-all(bf16[8,1,192,1536]{3,2,1,0:T(8,128)(2,1)} %bitcast.281), channel_id=1, replica_groups=mesh['rep'=4,'ep'=8] {'ep'}, dimensions={0} | all-to-all | bytes 9437184 | tf_op jit(solution)/shard_map/all_to_all | solution.py:130
  179.7 5.6 convert_bitcast_fusion
  190.7 123.1 %psum.64 = f32[]{:T(128)} all-reduce(f32[]{:T(128)} %convert_reduce_fusion), channel_id=1, replica_groups=mesh['rep'=4,'ep'=8] {'rep','ep'}, use_global_device_ids=true, to_apply=%region_15.16 | all-reduce | flops 1 | bytes 8 | tf_op jit(solution)/shard_map/psum | solution.py:71
  315.5 10.2 gather_fusion.1
  325.7 6.1 reshape.356
  341.9 7.8 mul.595
  354.7 12.7 %gather_fusion.2 = bf16[1536,1536]{1,0:T(8,128)(2,1)} fusion(bf16[1025,1536]{1,0:T(8,128)(2,1)} %concatenate.32, s32[2048]{0:T(1024)S(1)} %get-tuple-element.53), kind=kCustom, calls=%fused_computation.2 | custom fusion | bytes 9443328 | tf_op jit(solution)/shard_map/gather | solution.py:156
  367.4 108.5 %all_to_all.21 = bf16[8,1,192,1536]{3,2,1,0:T(8,128)(2,1)S(1)} all-to-all(bf16[8,1,192,1536]{3,2,1,0:T(8,128)(2,1)} %bitcast.282), channel_id=1, replica_groups=mesh['rep'=4,'ep'=8] {'ep'}, dimensions={0} | all-to-all | bytes 9437184 | tf_op jit(solution)/shard_map/all_to_all | solution.py:157
  478.1 5.2 fusion.39
  483.3 12.3 %fusion.45 = (bf16[8,192,768]{2,1,0:T(8,128)(2,1)S(1)}, bf16[8,1,192,768]{3,2,0,1:T(8,128)(2,1)S(1)}) fusion(f32[8,192,768]{2,1,0:T(8,128)} %copy-done.27, f32[8,192,768]{2,1,0:T(8,128)} %copy-done.26, bf16[1,768,1536]{2,1,0:T(8,128)(2,1)S(1)} %copy-done, bf16[8,1,192,1536]{3,2,1,0:T(8,128)(2,1)} %copy-done.25), kind=kOutput, calls=%fused_computation.72 | convolution fusion | flops 3652190208 | bytes 21233664 | tf_op jit(solution)/shard_map/secd,efd->secf/dot_general | solution.py:165
  499.6 5.9 fusion.23
  510.2 7.6 fusion.36
  519.5 7.7 fusion.33
  528.9 5.9 fusion.67
  535.0 78.5 %all-to-all-done.3 = bf16[8,1,192,1536]{3,2,1,0:T(8,128)(2,1)} async-done(((bf16[8,1,192,1536]{3,2,1,0:T(8,128)(2,1)}), bf16[8,1,192,1536]{3,2,1,0:T(8,128)(2,1)}, u32[]{:S(2)}, u32[]{:S(2)}) %all-to-all-start.3) | async-done | bytes 4718624 | tf_op jit(solution)/shard_map/all_to_all | solution.py:181
  613.4 10.6 %gather_fusion.3 = bf16[1024,1536]{1,0:T(8,128)(2,1)} fusion(bf16[1536,1536]{1,0:T(8,128)(2,1)} %bitcast.58, s32[1024]{0:T(1024)S(1)} %broadcast_clamp_fusion), kind=kCustom, calls=%fused_computation.3 | custom fusion | bytes 6295552 | tf_op jit(solution)/shard_map/gather | solution.py:182
  624.0 6.7 reshape.365
  630.7 7.8 reduce_sum.181
  682.4 30.2 %reduce-scatter.12.cloned.1.call-done = bf16[192,256]{1,0:T(8,128)(2,1)} async-done(((bf16[1536,256]{1,0:T(8,128)(2,1)}), bf16[192,256]{1,0:T(8,128)(2,1)}) %reduce-scatter.12.cloned.1.call-update) | async-done | bytes 98320 | tf_op jit(solution)/shard_map/reduce_scatter | solution.py:262
  712.6 65.2 %reduce-scatter.10.cloned.1.call-done = bf16[192,256]{1,0:T(8,128)(2,1)} async-done(((bf16[1536,256]{1,0:T(8,128)(2,1)}), bf16[192,256]{1,0:T(8,128)(2,1)}) %reduce-scatter.10.cloned.1.call-update) | async-done | bytes 98320 | tf_op jit(solution)/shard_map/reduce_scatter | solution.py:259
  777.7 98.2 %reduce-scatter.14.cloned.1.call-done = bf16[192,1536]{1,0:T(8,128)(2,1)} async-done(((bf16[1536,1536]{1,0:T(8,128)(2,1)}), bf16[192,1536]{1,0:T(8,128)(2,1)}) %reduce-scatter.14.cloned.1.call-update) | async-done | bytes 589840 | tf_op jit(solution)/shard_map/reduce_scatter | solution.py:265
  875.9 99.1 %reduce-scatter.8.cloned.1.call-done = bf16[192,1536]{1,0:T(8,128)(2,1)} async-done(((bf16[1536,1536]{1,0:T(8,128)(2,1)}), bf16[192,1536]{1,0:T(8,128)(2,1)}) %reduce-scatter.8.cloned.1.call-update) | async-done | bytes 589840 | tf_op jit(solution)/shard_map/reduce_scatter | solution.py:256
  975.7 42.2 %all-reduce.2 = (f32[]{:T(128)}, f32[1536]{0:T(1024)}, f32[1536]{0:T(1024)}, f32[1536,8]{0,1:T(8,128)}) all-reduce(f32[]{:T(128)} %multiply_reduce_fusion.4, f32[1536]{0:T(1024)S(1)} %get-tuple-element.15, f32[1536]{0:T(1024)S(1)} %copy-done.53, f32[1536,8]{0,1:T(8,128)S(1)} %fusion.125), channel_id=1, replica_groups=mesh['rep'=4,'ep'=8] {'rep','ep'}, use_global_device_ids=true, to_apply=%region_13.14 | all-reduce | flops 15361 | bytes 122888 | tf_op jit(solution)/shard_map/psum | solution.py:275
  (289 shorter events, 143.8 us)
Async XLA Ops:
  7.2 172.5 %copy-start = (bf16[1,768,1536]{2,1,0:T(8,128)(2,1)S(1)}, bf16[1,768,1536]{2,1,0:T(8,128)(2,1)}, u32[]{:S(2)}) copy-start(bf16[1,768,1536]{2,1,0:T(8,128)(2,1)} %param.29) | copy-start | bytes 7077892
  7.2 17.1 %copy-start.7 = (bf16[256,1536]{1,0:T(8,128)(2,1)S(1)}, bf16[256,1536]{1,0:T(8,128)(2,1)}, u32[]{:S(2)}) copy-start(bf16[256,1536]{1,0:T(8,128)(2,1)} %param.15) | copy-start | bytes 2359300
  10.6 19.4 %copy-start.55 = (f32[256]{0:T(256)}, f32[256]{0:T(256)S(1)}, u32[]{:S(2)}) copy-start(f32[256]{0:T(256)S(1)} %fusion.102) | copy-start | bytes 3076
  11.3 18.7 %copy-start.45 = (f32[1536]{0:T(1024)}, f32[1536]{0:T(1024)S(1)}, u32[]{:S(2)}) copy-start(f32[1536]{0:T(1024)S(1)} %convert_element_type.189) | copy-start | bytes 18436
  12.0 36.3 %copy-start.49 = (f32[1536]{0:T(1024)}, f32[1536]{0:T(1024)S(1)}, u32[]{:S(2)}) copy-start(f32[1536]{0:T(1024)S(1)} %convert_element_type.196) | copy-start | bytes 18436
  56.3 112.0 %copy-start.71 = (bf16[1,1536,768]{2,1,0:T(8,128)(2,1)S(1)}, bf16[1,1536,768]{2,1,0:T(8,128)(2,1)}, u32[]{:S(2)}) copy-start(bf16[1,1536,768]{2,1,0:T(8,128)(2,1)} %param.28) | copy-start | bytes 7077892
  185.3 128.5 %copy-start.17 = (bf16[256,1536]{1,0:T(8,128)(2,1)S(1)}, bf16[256,1536]{1,0:T(8,128)(2,1)}, u32[]{:S(2)}) copy-start(bf16[256,1536]{1,0:T(8,128)(2,1)} %copy-done.16) | copy-start | bytes 2359300
  185.3 128.5 %copy-start.51 = (bf16[1536,8]{0,1:T(8,128)(2,1)S(1)}, bf16[1536,8]{0,1:T(8,128)(2,1)}, u32[]{:S(2)}) copy-start(bf16[1536,8]{0,1:T(8,128)(2,1)} %param.26) | copy-start | bytes 73732
  185.3 128.8 %copy-start.52 = (s32[256,4]{0,1:T(4,128)S(1)}, s32[256,4]{0,1:T(4,128)}, u32[]{:S(2)}) copy-start(s32[256,4]{0,1:T(4,128)} %param.17) | copy-start | bytes 12292
  185.3 130.1 %copy-start.60 = (s32[1024,1]{0,1:T(1,128)S(1)}, s32[1024,1]{0,1:T(1,128)}, u32[]{:S(2)}) copy-start(s32[1024,1]{0,1:T(1,128)} %copy-done.59) | copy-start | bytes 12292
  185.3 130.1 %all-to-all-start.1 = ((bf16[8,1,192,1536]{3,2,1,0:T(8,128)(2,1)}), bf16[8,1,192,1536]{3,2,1,0:T(8,128)(2,1)}, u32[]{:S(2)}, u32[]{:S(2)}) async-start(bf16[8,1,192,1536]{3,2,1,0:T(8,128)(2,1)} %convert_bitcast_fusion), calls=%async_computation.1 | async-start | bytes 9437184 | tf_op jit(solution)/shard_map/all_to_all | solution.py:140
  190.1 478.9 %reduce-scatter.20.cloned.1.call-start = ((), (), s32[]{:S(2)}) async-start(), calls=%async_computation.17 | async-start | bytes 2949120 | tf_op jit(solution)/shard_map/reduce_scatter | solution.py:193
  367.4 110.6 %copy-start.31 = (bf16[8,192,768]{2,1,0:T(8,128)(2,1)S(1)}, bf16[8,192,768]{2,1,0:T(8,128)(2,1)}, u32[]{:S(2)}) copy-start(bf16[8,192,768]{2,1,0:T(8,128)(2,1)} %copy-done.30) | copy-start | bytes 7077892
  505.4 108.0 %all-to-all-start.3 = ((bf16[8,1,192,1536]{3,2,1,0:T(8,128)(2,1)}), bf16[8,1,192,1536]{3,2,1,0:T(8,128)(2,1)}, u32[]{:S(2)}, u32[]{:S(2)}) async-start(bf16[8,1,192,1536]{3,2,1,0:T(8,128)(2,1)} %fusion.23), calls=%async_computation.3 | async-start | bytes 9437184 | tf_op jit(solution)/shard_map/all_to_all | solution.py:181
  510.2 161.0 %reduce-scatter.18.cloned.1.call-start = ((), (), s32[]{:S(2)}) async-start(), calls=%async_computation.16 | async-start | bytes 2949120 | tf_op jit(solution)/shard_map/reduce_scatter | solution.py:190
  517.9 155.4 %reduce-scatter.16.cloned.1.call-start = ((), (), s32[]{:S(2)}) async-start(), calls=%async_computation.15 | async-start | bytes 2949120 | tf_op jit(solution)/shard_map/reduce_scatter | solution.py:187
  527.2 185.4 %reduce-scatter.12.cloned.1.call-start = ((), (), s32[]{:S(2)}) async-start(), calls=%async_computation.13 | async-start | bytes 884736 | tf_op jit(solution)/shard_map/reduce_scatter | solution.py:262
  650.4 127.4 %reduce-scatter.10.cloned.1.call-start = ((), (), s32[]{:S(2)}) async-start(), calls=%async_computation.12 | async-start | bytes 884736 | tf_op jit(solution)/shard_map/reduce_scatter | solution.py:259
  657.7 218.2 %reduce-scatter.14.cloned.1.call-start = ((), (), s32[]{:S(2)}) async-start(), calls=%async_computation.14 | async-start | bytes 5308416 | tf_op jit(solution)/shard_map/reduce_scatter | solution.py:265
  661.7 313.3 %reduce-scatter.8.cloned.1.call-start = ((), (), s32[]{:S(2)}) async-start(), calls=%async_computation.11 | async-start | bytes 5308416 | tf_op jit(solution)/shard_map/reduce_scatter | solution.py:256
  667.6 355.1 %all-reduce.6.cloned.1.call-start = ((), (), s32[]{:S(2)}) async-start(), calls=%async_computation.18 | async-start | bytes 2752512 | tf_op jit(solution)/shard_map/psum | solution.py:270
  680.5 294.5 %copy-start.66 = (f32[1,256]{1,0:T(1,128)S(1)}, f32[1,256]{1,0:T(1,128)}, u32[]{:S(2)}) copy-start(f32[1,256]{1,0:T(1,128)} %copy-done.65) | copy-start | bytes 3076
  680.5 294.5 %copy-start.67 = (f32[256]{0:T(256)S(1)}, f32[256]{0:T(256)}, u32[]{:S(2)}) copy-start(f32[256]{0:T(256)} %get-tuple-element.17) | copy-start | bytes 3076
  680.5 295.1 %copy-start.53 = (f32[1536]{0:T(1024)S(1)}, f32[1536]{0:T(1024)}, u32[]{:S(2)}) copy-start(f32[1536]{0:T(1024)} %get-tuple-element.13) | copy-start | bytes 18436
  (67 other events, 244.5 us)
Sparse Core Ops, SparseCore 0:
  483.4 32.2 reduce-scatter.19
  518.4 34.4 reduce-scatter.17
  555.4 33.0 reduce-scatter.15
  650.5 62.0 reduce-scatter.11
  716.3 61.3 reduce-scatter.9
  781.7 94.1 reduce-scatter.13
  880.0 94.9 reduce-scatter.7
  977.7 40.9 all-reduce.5
where the time goes:
time: 1050 us; the launch traced here: 1040 us
  blocking collectives  386 us (37%)
  waiting for transfers between devices  371 us (35%)
  matrix products  108 us (10%)
  local copies, waits for them, and re-layouts  99.2 us (9%)
  other arithmetic  44.7 us (4%)
  between operations  18.6 us (2%)
    psum x1, blocking collectives, shards(): count_total = lax.psum(jnp.sum(valid_rows), ('rep', 'ep'))  123 us
    all_to_all x1, blocking collectives, shards(): lax.all_to_all(send_rows, 'ep', split_axis=0, concat_axis=0, tiled=True)  112 us
    all_to_all x1, blocking collectives, shards(): lax.all_to_all(send_grad, 'ep', split_axis=0, concat_axis=0, tiled=True)  108 us
    reduce_scatter x1, waiting for transfers between devices, shards(): lax.psum_scatter(attn_grads[0].astype(jnp.bfloat16), 'ep', scatter_dimens...  99.1 us
    reduce_scatter x1, waiting for transfers between devices, shards(): lax.psum_scatter(attn_grads[3].astype(jnp.bfloat16), 'ep', scatter_dimens...  98.2 us
    all_to_all x1, waiting for transfers between devices, shards(): lax.all_to_all(grad_rows, 'ep', split_axis=0, concat_axis=0, tiled=True)  78.5 us
    reduce_scatter x1, waiting for transfers between devices, shards(): lax.psum_scatter(attn_grads[1].astype(jnp.bfloat16), 'ep', scatter_dimens...  65.2 us
    psum x1, blocking collectives, shards(): lax.psum((grad_router, grad_gain_one, grad_gain_two, numerator), ('rep',...  42.2 us
  transfers between devices with their start and end apart: 10, of which 5 were waited for; matrix products, arithmetic and copies ran while one was open for 11% of the time, Pallas kernels for 0%

commit v1 on v0

v1 whole, which is shorter than its diff:
```python
import functools

import jax
import jax.numpy as jnp
from jax import lax
from jax.sharding import Mesh
from jax.sharding import PartitionSpec as P

H = 12
KVH = 2
HEAD = 128

EPSILON = 1e-06
ROPE_BASE = 10000.0
NEG_FILL = -1e30
ALL = ("x", "c", "z", "y")
EP = ("z", "y")
F32 = jnp.float32
BF16 = jnp.bfloat16
RING_LIMIT = 16


def dot(a, b, dims=((1,), (0,))):
    return lax.dot_general(a, b, (dims, ((), ())), preferred_element_type=F32)


def dot_nt(a, b):
    return dot(a, b, ((1,), (1,)))


def dot_tn(a, b):
    return dot(a, b, ((0,), (0,)))


def rms_norm(values, gain):
    inverse = lax.rsqrt(jnp.mean(values * values, axis=-1, keepdims=True) + EPSILON)
    return values * inverse * gain


def rotate(values, direction):
    length = values.shape[-3]
    half_dim = values.shape[-1] // 2
    frequency = ROPE_BASE ** (-jnp.arange(half_dim, dtype=F32) / half_dim)
    angles = jnp.arange(length, dtype=F32)[:, None] * frequency[None, :] * direction
    cosine = jnp.cos(angles)[:, None, :]
    sinusoid = jnp.sin(angles)[:, None, :]
    first_half = values[..., :half_dim]
    second_half = values[..., half_dim:]
    return jnp.concatenate(
        [
            first_half * cosine - second_half * sinusoid,
            second_half * cosine + first_half * sinusoid,
        ],
        axis=-1,
    )


def activate(gate_pre, up_pre):
    return jax.nn.gelu(gate_pre, approximate=True) * up_pre


class Ring:
    def __init__(self, z_size, y_size):
        cycle = [(z, 0) for z in range(z_size)]
        for step, z in enumerate(reversed(range(z_size))):
            rest = list(range(1, y_size))
            cycle += [(z, y) for y in (rest if step % 2 == 0 else rest[::-1])]
        self.order = [z * y_size + y for z, y in cycle]
        self.size = len(self.order)
        self.half = self.size // 2
        n = self.size
        self.forward = [(self.order[i], self.order[(i + 1) % n]) for i in range(n)]
        self.backward = [(b, a) for a, b in self.forward]
        self.place = [self.order.index(e) for e in range(n)]

    def fwd(self, a):
        return lax.ppermute(a, EP, self.forward)

    def bwd(self, a):
        return lax.ppermute(a, EP, self.backward)

    def owners(self):
        mine = jnp.asarray(self.place, jnp.int32)[lax.axis_index(EP)]
        behind = (mine - jnp.arange(self.size, dtype=jnp.int32)) % self.size
        return jnp.asarray(self.order, jnp.int32)[behind]

    def gather(self, a):
        blocks = [None] * self.size
        blocks[0] = a
        ahead = behind = a
        for s in range(1, self.half):
            ahead = self.fwd(ahead)
            behind = self.bwd(behind)
            blocks[s] = ahead
            blocks[self.size - s] = behind
        rows = a.shape[0] // 2
        blocks[self.half] = jnp.concatenate([self.fwd(ahead[:rows]), self.bwd(behind[rows:])], axis=0)
        return blocks

    def scatter_sum(self, terms):
        far = terms(self.half)
        rows = far.shape[0] // 2
        down = self.bwd(far[:rows])
        up = self.fwd(far[rows:])
        first, last = terms(self.half - 1), terms(self.half + 1)

        def add(a, b):
            return (a.astype(F32) + b.astype(F32)).astype(BF16)

        down = jnp.concatenate([add(first[:rows], down), first[rows:]], axis=0)
        up = jnp.concatenate([last[:rows], add(last[rows:], up)], axis=0)
        for s in range(self.half - 2, 0, -1):
            down = add(self.bwd(down), terms(s))
            up = add(self.fwd(up), terms(self.size - s))
        down = self.bwd(down)
        up = self.fwd(up)
        return down.astype(F32) + up.astype(F32) + terms(0).astype(F32)


def butterfly_sum(a, axes):
    for axis in axes:
        size = lax.axis_size(axis)
        step = 1
        while step < size:
            a = a + lax.ppermute(a, axis, [(i, i ^ step) for i in range(size)])
            step *= 2
    return a


def scatter_axis(a, axis, dim):
    size = lax.axis_size(axis)
    if size != 2:
        return lax.psum_scatter(a, axis, scatter_dimension=dim, tiled=True).astype(F32)
    me = lax.axis_index(axis)
    share = a.shape[dim] // 2
    mine = lax.dynamic_slice_in_dim(a, me * share, share, dim)
    other = lax.dynamic_slice_in_dim(a, (1 - me) * share, share, dim)
    got = lax.ppermute(other, axis, [(0, 1), (1, 0)])
    return mine.astype(F32) + got.astype(F32)


def gather_axis(a, axis, dim):
    size = lax.axis_size(axis)
    if size != 2:
        return lax.all_gather(a, axis, axis=dim, tiled=True)
    got = lax.ppermute(a, axis, [(0, 1), (1, 0)])
    first = lax.axis_index(axis) == 0
    return jnp.concatenate([jnp.where(first, a, got), jnp.where(first, got, a)], axis=dim)


class RingExperts:
    def __init__(self, ring, owners, moe_in, route_hot, gate_weights, top, w_gate, w_up, w_down):
        self.ring, self.owners, self.moe_in = ring, owners, moe_in
        self.weights = (w_gate, w_up, w_down)
        gates = lax.all_to_all(gate_weights.T, EP, 0, 0, tiled=True)
        self.gates = jnp.take(gates, owners, axis=0).T
        n = ring.size
        self.by_distance = sorted(range(n), key=lambda j: min(j, n - j))

    def forward(self):
        w_gate, w_up, w_down = self.weights
        self.rows_in = self.ring.gather(self.moe_in)
        self.gate_pre, self.up_pre, self.hidden = {}, {}, {}

        def term(j):
            gate_pre = dot(self.rows_in[j], w_gate)
            up_pre = dot(self.rows_in[j], w_up)
            self.hidden[j] = activate(gate_pre, up_pre).astype(BF16)
            self.gate_pre[j], self.up_pre[j] = gate_pre.astype(BF16), up_pre.astype(BF16)
            return (dot(self.hidden[j], w_down) * self.gates[:, j : j + 1]).astype(BF16)

        terms = {j: term(j) for j in self.by_distance}
        return self.ring.scatter_sum(terms.get)

    def backward(self, grad_out):
        w_gate, w_up, w_down = self.weights
        grads_in = self.ring.gather(grad_out.astype(BF16))
        gate_lows, up_lows, scaled, dots = {}, {}, {}, {}

        def term(j):
            raw = dot_nt(grads_in[j], w_down)
            hidden = self.hidden[j].astype(F32)
            dots[j] = jnp.sum(raw * hidden, axis=1)
            gate = self.gates[:, j : j + 1]
            _, pull = jax.vjp(activate, self.gate_pre[j].astype(F32), self.up_pre[j].astype(F32))
            grad_gate, grad_up = pull(raw * gate)
            gate_lows[j], up_lows[j] = grad_gate.astype(BF16), grad_up.astype(BF16)
            scaled[j] = (hidden * gate).astype(BF16)
            return (dot_nt(gate_lows[j], w_gate) + dot_nt(up_lows[j], w_up)).astype(BF16)

        terms = {j: term(j) for j in self.by_distance}
        stacked = jnp.stack([dots[j] for j in range(self.ring.size)])
        back = jnp.zeros_like(stacked).at[self.owners].set(stacked)
        grad_gates = lax.all_to_all(back, EP, 0, 0, tiled=True).T
        grad_moe_in = self.ring.scatter_sum(terms.get)

        def joined(parts):
            return jnp.concatenate([parts[j] for j in range(self.ring.size)], axis=0)

        rows_all = joined(self.rows_in)
        expert_grads = [
            dot_tn(rows_all, joined(gate_lows)).astype(BF16),
            dot_tn(rows_all, joined(up_lows)).astype(BF16),
            dot_tn(joined(scaled), joined(grads_in)).astype(BF16),
        ]
        return grad_moe_in, grad_gates, expert_grads


class SlotExperts:
    def __init__(self, ring, owners, moe_in, route_hot, gate_weights, top, w_gate, w_up, w_down):
        rows, experts = route_hot.shape
        self.slots = 3 * rows * top // (2 * experts)
        self.group = ring.size
        self.moe_in, self.weights = moe_in, (w_gate, w_up, w_down)
        places = jnp.arange(rows)
        earlier = (places[:, None] > places[None, :]).astype(BF16)
        rank = dot(earlier, route_hot.astype(BF16)).T[:, None, :]
        slot = jnp.arange(self.slots, dtype=F32)[None, :, None]
        picks = ((rank == slot) & route_hot.T[:, None, :]).reshape(experts * self.slots, rows)
        self.picks = picks.astype(BF16)
        self.slot_gate = jnp.where(picks, jnp.repeat(gate_weights.T, self.slots, axis=0), 0.0)

    def swap(self, rows):
        blocks = rows.reshape(self.group, -1, rows.shape[1])
        return lax.all_to_all(blocks, EP, 0, 0, tiled=True).reshape(rows.shape)

    def forward(self):
        w_gate, w_up, w_down = self.weights
        self.arrived = self.swap(dot(self.picks, self.moe_in).astype(BF16))
        self.gate_pre = dot(self.arrived, w_gate)
        self.up_pre = dot(self.arrived, w_up)
        self.hidden = activate(self.gate_pre, self.up_pre).astype(BF16)
        self.returned = self.swap(dot(self.hidden, w_down).astype(BF16))
        return jnp.dot(self.slot_gate.T, self.returned.astype(F32), precision=lax.Precision.HIGHEST)

    def backward(self, grad_out):
        w_gate, w_up, w_down = self.weights
        grad_low = grad_out.astype(BF16)
        rows, experts = grad_out.shape[0], self.picks.shape[0] // self.slots
        products = dot_nt(grad_low, self.returned) * self.picks.T.astype(F32)
        grad_gates = jnp.sum(products.reshape(rows, experts, self.slots), axis=2)
        slot_gate = jnp.sum(self.slot_gate, axis=1, keepdims=True)
        grads_in = self.swap((dot(self.picks, grad_low) * slot_gate).astype(BF16))
        _, pull = jax.vjp(activate, self.gate_pre, self.up_pre)
        grad_gate, grad_up = pull(dot_nt(grads_in, w_down))
        gate_low, up_low = grad_gate.astype(BF16), grad_up.astype(BF16)
        back = self.swap((dot_nt(gate_low, w_gate) + dot_nt(up_low, w_up)).astype(BF16))
        expert_grads = [
            dot_tn(self.arrived, gate_low).astype(BF16),
            dot_tn(self.arrived, up_low).astype(BF16),
            dot_tn(self.hidden, grads_in).astype(BF16),
        ]
        return dot_tn(self.picks, back), grad_gates, expert_grads


def shards(
    ring,
    tokens,
    segments,
    routes,
    valid_mask,
    teacher,
    gain_one,
    w_query,
    w_key,
    w_value,
    w_out,
    gain_two,
    router,
    w_gate,
    w_up,
    w_down,
):
    length = tokens.shape[0]
    width = tokens.shape[1]
    experts_all = router.shape[1]
    tokens_all = length * lax.axis_size(ALL)
    groups = H // KVH
    score_scale = HEAD ** (-0.5)
    w_gate, w_up, w_down = w_gate[0], w_up[0], w_down[0]
    valid_rows = valid_mask.reshape(length).astype(F32)
    count_total = butterfly_sum(jnp.full((8, 128), jnp.sum(valid_rows), F32), ("c", "x", "y", "z"))[0, 0]
    token_values = tokens.astype(F32)
    normed_one, norm_one_pull = jax.vjp(rms_norm, token_values, gain_one.astype(F32))
    normed_low = normed_one.astype(BF16)
    query_pre = dot(normed_low, w_query).reshape(length, H, HEAD)
    key_pre = dot(normed_low, w_key).reshape(length, KVH, HEAD)
    value_low = dot(normed_low, w_value).astype(BF16).reshape(length, KVH, HEAD)
    query_rot = rotate(query_pre, 1.0).astype(BF16).reshape(length, KVH, groups, HEAD)
    key_rot = rotate(key_pre, 1.0).astype(BF16)
    places = jnp.arange(length)
    seg_row = segments.reshape(length)
    allowed = (seg_row[:, None] == seg_row[None, :]) & (places[:, None] >= places[None, :])

    def masked_scores():
        raw_scores = jnp.einsum("qkgc,pkc->kgqp", query_rot, key_rot, preferred_element_type=F32)
        return jnp.where(allowed, raw_scores * score_scale, NEG_FILL)

    scores = masked_scores()
    row_peak = jnp.max(scores, axis=-1, keepdims=True)
    exp_terms = jnp.exp(scores - row_peak)
    row_total = jnp.sum(exp_terms, axis=-1, keepdims=True)
    log_total = row_peak + jnp.log(row_total)
    weights_low = (exp_terms / row_total).astype(BF16)
    context = jnp.einsum("kgqp,pkc->qkgc", weights_low, value_low, preferred_element_type=F32)
    context = context.reshape(length, H * HEAD).astype(BF16)
    mixed_rows = token_values + dot(context, w_out)
    normed_two, norm_two_pull = jax.vjp(rms_norm, mixed_rows, gain_two.astype(F32))
    moe_in = normed_two.astype(BF16)
    logits = dot(moe_in, router)
    expert_ids = jnp.arange(experts_all, dtype=jnp.int32)
    route_hot = jnp.any(routes[:, :, None] == expert_ids[None, None, :], axis=1)
    peak = jnp.max(jnp.where(route_hot, logits, -jnp.inf), axis=1, keepdims=True)
    gate_terms = jnp.where(route_hot, jnp.exp(jnp.where(route_hot, logits - peak, 0.0)), 0.0)
    gate_weights = gate_terms / jnp.sum(gate_terms, axis=1, keepdims=True)

    owners = ring.owners()
    form = RingExperts if ring.size <= RING_LIMIT else SlotExperts
    experts = form(ring, owners, moe_in, route_hot, gate_weights, routes.shape[1], w_gate, w_up, w_down)
    moe_out = experts.forward()
    output_rows = mixed_rows + moe_out
    residual_gap = output_rows - teacher.astype(F32)
    numerator = jnp.sum(valid_rows * jnp.sum(residual_gap * residual_gap, axis=-1))
    grad_out = 2.0 * tokens_all / count_total * valid_rows[:, None] * residual_gap

    grad_moe_in, grad_gates, expert_grads = experts.backward(grad_out)
    x_size, c_size = lax.axis_size("x"), lax.axis_size("c")
    shares = []
    for g in expert_grads:
        part = g.reshape(x_size, c_size, -1, g.shape[1])
        part = scatter_axis(part, "c", 1).astype(BF16)
        shares.append(scatter_axis(part, "x", 0).reshape(1, -1, g.shape[1]))

    grad_chosen = gate_weights * (grad_gates - jnp.sum(gate_weights * grad_gates, axis=1, keepdims=True))
    grad_logits = grad_chosen.astype(BF16)
    grad_router = dot_tn(moe_in, grad_logits)
    grad_moe_in = grad_moe_in + dot_nt(grad_logits, router)
    grad_norm_two, grad_gain_two = norm_two_pull(grad_moe_in)
    grad_mixed = grad_out + grad_norm_two
    grad_branch = grad_mixed.astype(BF16)
    grad_w_out = dot_tn(context, grad_branch)
    grad_context = dot_nt(grad_branch, w_out)
    grad_context = grad_context.astype(BF16).reshape(length, KVH, groups, HEAD)
    attn_weights = jnp.exp(masked_scores() - log_total)
    grad_weights = jnp.einsum("qkgc,pkc->kgqp", grad_context, value_low, preferred_element_type=F32)
    row_term = jnp.sum(attn_weights * grad_weights, axis=-1, keepdims=True)
    grad_scores = (attn_weights * (grad_weights - row_term)).astype(BF16)
    grad_query_rot = jnp.einsum("kgqp,pkc->qkgc", grad_scores, key_rot, preferred_element_type=F32) * score_scale
    grad_key_rot = jnp.einsum("kgqp,qkgc->pkc", grad_scores, query_rot, preferred_element_type=F32) * score_scale
    grad_value = jnp.einsum("kgqp,qkgc->pkc", attn_weights.astype(BF16), grad_context, preferred_element_type=F32)
    grad_value = grad_value.astype(BF16).reshape(length, KVH * HEAD)
    grad_query = rotate(grad_query_rot.reshape(length, H, HEAD), -1.0).astype(BF16).reshape(length, H * HEAD)
    grad_key = rotate(grad_key_rot, -1.0).astype(BF16).reshape(length, KVH * HEAD)
    grad_qkv = jnp.concatenate([grad_query, grad_key, grad_value], axis=1)
    grad_w_qkv = dot_tn(normed_low, grad_qkv)
    grad_normed = dot_nt(grad_query, w_query) + dot_nt(grad_key, w_key) + dot_nt(grad_value, w_value)
    grad_norm_one, grad_gain_one = norm_one_pull(grad_normed)
    grad_tokens = grad_mixed + grad_norm_one

    n = ring.size

    def reduce_rows(g):
        cols = g.shape[1]
        part = g.astype(BF16).reshape(n, c_size, -1, cols)
        part = scatter_axis(part, "c", 1)
        part = part.astype(BF16).reshape(n, x_size, -1, cols)
        part = scatter_axis(part, "x", 1).astype(BF16).reshape(n, -1, cols)
        total = ring.scatter_sum(lambda j: lax.dynamic_index_in_dim(part, owners[j], 0, keepdims=False)).astype(BF16)
        total = gather_axis(gather_axis(total, "x", 0), "c", 0)
        return total.astype(F32)

    out_share = reduce_rows(grad_w_out)
    qkv_share = reduce_rows(grad_w_qkv)
    small = jnp.concatenate([grad_router.reshape(-1), grad_gain_two, jnp.full((128,), numerator)]).reshape(-1, 128)
    small = butterfly_sum(small, ("c", "x", "y", "z"))
    flat = small.reshape(-1)
    router_size = width * experts_all
    gain_one_sum = butterfly_sum(grad_gain_one.reshape(-1, 128), ("c", "x", "y", "z")).reshape(-1)
    return (
        output_rows.astype(BF16),
        flat[router_size + width] / count_total,
        grad_tokens,
        gain_one_sum,
        qkv_share[:, : H * HEAD],
        qkv_share[:, H * HEAD : (H + KVH) * HEAD],
        qkv_share[:, (H + KVH) * HEAD :],
        out_share,
        flat[router_size : router_size + width],
        flat[:router_size].reshape(width, experts_all),
        shares[0],
        shares[1],
        shares[2],
    )


def solution(mesh):
    rep, ep = mesh.shape["rep"], mesh.shape["ep"]
    x_size = rep // 2
    y_size = x_size if ep % x_size == 0 else 1
    grid = Mesh(mesh.devices.reshape(x_size, 2, ep // y_size, y_size), ALL)
    rows = P(ALL, None)
    whole = P()
    expert = P(EP, None, None)
    return jax.shard_map(
        functools.partial(shards, Ring(ep // y_size, y_size)),
        mesh=grid,
        in_specs=(rows,) * 5 + (whole,) * 7 + (expert,) * 3,
        out_specs=(rows, whole, rows, whole)
        + (P(EP, None),) * 4
        + (whole, whole)
        + (P(EP, ("x", "c"), None),) * 3,
        check_vma=False,
    )
```

time: 1050 us -> 562 us (0.54)
  blocking collectives: 386 us -> 0 us
  waiting for transfers between devices: 371 us -> 206 us
  starting transfers between devices: 9.99 us -> 91.3 us
  local copies, waits for them, and re-layouts: 99.2 us -> 61.1 us
  matrix products: 108 us -> 120 us
    reduce_scatter x7 -> x0, waiting for transfers between devices: 293 us -> none  [the longest x1 99.1 us: shards(): lax.psum_scatter(attn_grads[0].astype(jnp.bfloat16), 'ep', scatter_dimens...]
    all_to_all x2 -> x0, blocking collectives: 220 us -> none  [the longest x1 112 us: shards(): lax.all_to_all(send_rows, 'ep', split_axis=0, concat_axis=0, tiled=True)]
    ppermute x0 -> x77, waiting for transfers between devices: none -> 206 us  [the longest x24 110 us: fwd(): return lax.ppermute(a, EP, self.forward)]
    psum x2 -> x0, blocking collectives: 165 us -> none  [the longest x1 123 us: shards(): count_total = lax.psum(jnp.sum(valid_rows), ('rep', 'ep'))]
    ppermute x0 -> x77, starting transfers between devices: none -> 81.2 us  [the longest x24 29 us: fwd(): return lax.ppermute(a, EP, self.forward)]
    all_to_all x2, waiting for transfers between devices: 78.5 us -> 0.01 us  [the longest x1 0.01 us: backward(): grad_gates = lax.all_to_all(back, EP, 0, 0, tiled=True).T]
    gather x4 -> x2, local copies, waits for them, and re-layouts: 39.8 us -> 1.2 us  [the longest x1 0.64 us: owners(): return jnp.asarray(self.order, jnp.int32)[behind]]
    dot_general x28 -> x66, matrix products: 103 us -> 117 us  [the longest x64 112 us: dot(): return lax.dot_general(a, b, (dims, ((), ())), preferred_element_type=F32)]
  transfers between devices with their start and end apart: 10 -> 79, of which waited for: 5 -> 38; matrix products, arithmetic and copies ran while one was open for 11% -> 31% of each run, Pallas kernels for 0% -> 0%
where the time goes in v1:
time: 562 us; the launch traced here: 552 us
  waiting for transfers between devices  206 us (37%)
  matrix products  120 us (21%)
  starting transfers between devices  91.3 us (16%)
  local copies, waits for them, and re-layouts  61.1 us (11%)
  other arithmetic  51.5 us (9%)
  between operations  21.8 us (4%)
    dot_general x64, matrix products, dot(): return lax.dot_general(a, b, (dims, ((), ())), preferred_element_type=F32)  112 us
    ppermute x24, waiting for transfers between devices, fwd(): return lax.ppermute(a, EP, self.forward)  110 us
    ppermute x24, waiting for transfers between devices, bwd(): return lax.ppermute(a, EP, self.backward)  45.7 us
    ppermute x10, waiting for transfers between devices, scatter_axis(): got = lax.ppermute(other, axis, [(0, 1), (1, 0)])  37.1 us
    unnamed x296, local copies, waits for them, and re-layouts  30.4 us
    ppermute x24, starting transfers between devices, fwd(): return lax.ppermute(a, EP, self.forward)  29 us
    ppermute x24, starting transfers between devices, bwd(): return lax.ppermute(a, EP, self.backward)  23.5 us
    ppermute x15, starting transfers between devices, butterfly_sum(): a = a + lax.ppermute(a, axis, [(i, i ^ step) for i in range(size)])  20 us
  transfers between devices with their start and end apart: 79, of which 38 were waited for; matrix products, arithmetic and copies ran while one was open for 31% of the time, Pallas kernels for 0%

profile of v1, /device:TPU:0, one launch (start us, length us, event | category | flops | bytes accessed | tf_op | source)
XLA Modules:
  0.0 552.1 jit_solution(6565343607359407661)
XLA Ops:
  13.9 4.4 fusion.370
  40.6 6.3 %all-to-all-start = ((f32[8,1,256]{2,1,0:T(1,128)}), f32[8,1,256]{2,1,0:T(1,128)S(1)}, u32[]{:S(2)}, u32[]{:S(2)}) async-start(f32[8,1,256]{2,1,0:T(1,128)} %copy.128), calls=%async_computation | async-start | bytes 16384 | tf_op jit(solution)/shard_map/all_to_all | solution.py:155
  49.5 3.6 fusion.95
  101.8 9.3 %collective-permute-done.5 = bf16[256,1536]{1,0:T(8,128)(2,1)S(1)} collective-permute-done((bf16[256,1536]{1,0:T(8,128)(2,1)}, bf16[256,1536]{1,0:T(8,128)(2,1)S(1)}, u32[]{:S(2)}, u32[]{:S(2)}) %collective-permute-start.5) | collective-permute-done | bytes 786464 | tf_op jit(solution)/shard_map/ppermute | solution.py:80
  117.5 11.3 %collective-permute-done.6 = bf16[256,1536]{1,0:T(8,128)(2,1)S(1)} collective-permute-done((bf16[256,1536]{1,0:T(8,128)(2,1)S(1)}, bf16[256,1536]{1,0:T(8,128)(2,1)S(1)}, u32[]{:S(2)}, u32[]{:S(2)}) %collective-permute-start.6) | collective-permute-done | bytes 786464 | tf_op jit(solution)/shard_map/ppermute | solution.py:80
  153.0 6.2 %collective-permute-done.12 = bf16[128,1536]{1,0:T(8,128)(2,1)S(1)} collective-permute-done((bf16[128,1536]{1,0:T(8,128)(2,1)S(1)}, bf16[128,1536]{1,0:T(8,128)(2,1)S(1)}, u32[]{:S(2)}, u32[]{:S(2)}) %collective-permute-start.12) | collective-permute-done | bytes 393248 | tf_op jit(solution)/shard_map/ppermute | solution.py:77
  162.4 14.4 %collective-permute-done.13 = bf16[256,1536]{1,0:T(8,128)(2,1)S(1)} collective-permute-done((bf16[256,1536]{1,0:T(8,128)(2,1)S(1)}, bf16[256,1536]{1,0:T(8,128)(2,1)S(1)}, u32[]{:S(2)}, u32[]{:S(2)}) %collective-permute-start.13) | collective-permute-done | bytes 786464 | tf_op jit(solution)/shard_map/ppermute | solution.py:77
  180.1 15.2 %collective-permute-done.14 = bf16[256,1536]{1,0:T(8,128)(2,1)S(1)} collective-permute-done((bf16[256,1536]{1,0:T(8,128)(2,1)S(1)}, bf16[256,1536]{1,0:T(8,128)(2,1)S(1)}, u32[]{:S(2)}, u32[]{:S(2)}) %collective-permute-start.14) | collective-permute-done | bytes 786464 | tf_op jit(solution)/shard_map/ppermute | solution.py:77
  202.0 8.4 %collective-permute-done.15 = bf16[256,1536]{1,0:T(8,128)(2,1)S(1)} collective-permute-done((bf16[256,1536]{1,0:T(8,128)(2,1)S(1)}, bf16[256,1536]{1,0:T(8,128)(2,1)S(1)}, u32[]{:S(2)}, u32[]{:S(2)}) %collective-permute-start.15) | collective-permute-done | bytes 786464 | tf_op jit(solution)/shard_map/ppermute | solution.py:77
  222.2 14.0 %collective-permute-done.21 = bf16[256,1536]{1,0:T(8,128)(2,1)S(1)} collective-permute-done((bf16[256,1536]{1,0:T(8,128)(2,1)S(1)}, bf16[256,1536]{1,0:T(8,128)(2,1)S(1)}, u32[]{:S(2)}, u32[]{:S(2)}) %collective-permute-start.21) | collective-permute-done | bytes 786464 | tf_op jit(solution)/shard_map/ppermute | solution.py:77
  245.2 10.4 %collective-permute-done.22 = bf16[256,1536]{1,0:T(8,128)(2,1)S(1)} collective-permute-done((bf16[256,1536]{1,0:T(8,128)(2,1)S(1)}, bf16[256,1536]{1,0:T(8,128)(2,1)S(1)}, u32[]{:S(2)}, u32[]{:S(2)}) %collective-permute-start.22) | collective-permute-done | bytes 786464 | tf_op jit(solution)/shard_map/ppermute | solution.py:77
  265.2 7.4 %collective-permute-done.27 = bf16[256,1536]{1,0:T(8,128)(2,1)S(1)} collective-permute-done((bf16[256,1536]{1,0:T(8,128)(2,1)S(1)}, bf16[256,1536]{1,0:T(8,128)(2,1)S(1)}, u32[]{:S(2)}, u32[]{:S(2)}) %collective-permute-start.27) | collective-permute-done | bytes 786464 | tf_op jit(solution)/shard_map/ppermute | solution.py:80
  287.6 3.7 all-to-all-start.1
  298.2 9.1 %convolution_convert_fusion.2 = bf16[768,1536]{1,0:T(8,128)(2,1)S(1)} fusion(bf16[2048,768]{1,0:T(8,128)(2,1)S(1)} %copy-done.130, bf16[2048,1536]{1,0:T(8,128)(2,1)} %constant_dynamic-update-slice_fusion.27), kind=kOutput, calls=%fused_computation.7 | convolution fusion | flops 4833017856 | bytes 11796480 | tf_op jit(solution)/shard_map/dot_general | solution.py:24
  314.0 5.5 convolution_convert_fusion.3
  319.5 5.7 %convolution_convert_fusion.4 = bf16[1536,768]{1,0:T(8,128)(2,1)S(1)} fusion(bf16[2048,1536]{1,0:T(8,128)(2,1)S(1)} %bitcast.470, bf16[2048,768]{1,0:T(8,128)(2,1)S(1)} %get-tuple-element.129), kind=kOutput, calls=%fused_computation.9 | convolution fusion | flops 4833017856 | bytes 11796480 | tf_op jit(solution)/shard_map/dot_general | solution.py:24
  357.4 9.7 %collective-permute-done.34 = bf16[256,1536]{1,0:T(8,128)(2,1)S(1)} collective-permute-done((bf16[256,1536]{1,0:T(8,128)(2,1)S(1)}, bf16[256,1536]{1,0:T(8,128)(2,1)S(1)}, u32[]{:S(2)}, u32[]{:S(2)}) %collective-permute-start.34) | collective-permute-done | bytes 786464 | tf_op jit(solution)/shard_map/ppermute | solution.py:77
  372.0 13.0 %collective-permute-done.35 = bf16[256,1536]{1,0:T(8,128)(2,1)S(1)} collective-permute-done((bf16[256,1536]{1,0:T(8,128)(2,1)S(1)}, bf16[256,1536]{1,0:T(8,128)(2,1)S(1)}, u32[]{:S(2)}, u32[]{:S(2)}) %collective-permute-start.35) | collective-permute-done | bytes 786464 | tf_op jit(solution)/shard_map/ppermute | solution.py:77
  393.2 9.0 %collective-permute-done.36 = bf16[256,1536]{1,0:T(8,128)(2,1)S(1)} collective-permute-done((bf16[256,1536]{1,0:T(8,128)(2,1)S(1)}, bf16[256,1536]{1,0:T(8,128)(2,1)S(1)}, u32[]{:S(2)}, u32[]{:S(2)}) %collective-permute-start.36) | collective-permute-done | bytes 786464 | tf_op jit(solution)/shard_map/ppermute | solution.py:77
  460.0 16.6 %collective-permute-done.60 = bf16[8,1,48,1536]{3,2,1,0:T(8,128)(2,1)S(1)} collective-permute-done((bf16[8,1,48,1536]{3,2,1,0:T(8,128)(2,1)S(1)}, bf16[8,1,48,1536]{3,2,1,0:T(8,128)(2,1)S(1)}, u32[]{:S(2)}, u32[]{:S(2)}) %collective-permute-start.60) | collective-permute-done | bytes 1179680 | tf_op jit(solution)/shard_map/ppermute | solution.py:138
  487.3 20.5 %collective-permute-done.48 = bf16[8,1,48,2048]{3,2,1,0:T(8,128)(2,1)} collective-permute-done((bf16[8,1,48,2048]{3,2,1,0:T(8,128)(2,1)}, bf16[8,1,48,2048]{3,2,1,0:T(8,128)(2,1)}, u32[]{:S(2)}, u32[]{:S(2)}) %collective-permute-start.48) | collective-permute-done | bytes 1572896 | tf_op jit(solution)/shard_map/ppermute | solution.py:138
  528.6 4.8 collective-permute-done.51
  536.3 3.6 collective-permute-done.52
  541.3 5.1 collective-permute-done.57
  (663 shorter events, 313.2 us)
Async XLA Ops:
  34.1 58.8 %collective-permute-start.4 = (bf16[256,1536]{1,0:T(8,128)(2,1)}, bf16[256,1536]{1,0:T(8,128)(2,1)}, u32[]{:S(2)}, u32[]{:S(2)}) collective-permute-start(bf16[256,1536]{1,0:T(8,128)(2,1)} %get-tuple-element.121), channel_id=1, source_target_pairs={{2,0},{4,2},{6,4},{7,6},{5,7},{3,5},{1,3},{0,1},{10,8},{12,10},{14... | collective-permute-start | bytes 2359304 | tf_op jit(solution)/shard_map/ppermute | solution.py:80
  37.0 52.1 %collective-permute-start = (bf16[256,1536]{1,0:T(8,128)(2,1)}, bf16[256,1536]{1,0:T(8,128)(2,1)}, u32[]{:S(2)}, u32[]{:S(2)}) collective-permute-start(bf16[256,1536]{1,0:T(8,128)(2,1)} %get-tuple-element.121), channel_id=1, source_target_pairs={{0,2},{2,4},{4,6},{6,7},{7,5},{5,3},{3,1},{1,0},{8,10},{10,12},{12... | collective-permute-start | bytes 2359304 | tf_op jit(solution)/shard_map/ppermute | solution.py:77
  40.6 37.6 %all-to-all-start = ((f32[8,1,256]{2,1,0:T(1,128)}), f32[8,1,256]{2,1,0:T(1,128)S(1)}, u32[]{:S(2)}, u32[]{:S(2)}) async-start(f32[8,1,256]{2,1,0:T(1,128)} %copy.128), calls=%async_computation | async-start | bytes 16384 | tf_op jit(solution)/shard_map/all_to_all | solution.py:155
  89.1 24.0 %collective-permute-start.1 = (bf16[256,1536]{1,0:T(8,128)(2,1)}, bf16[256,1536]{1,0:T(8,128)(2,1)S(1)}, u32[]{:S(2)}, u32[]{:S(2)}) collective-permute-start(bf16[256,1536]{1,0:T(8,128)(2,1)} %collective-permute-done), channel_id=1, source_target_pairs={{0,2},{2,4},{4,6},{6,7},{7,5},{5,3},{3,1},{1,0},{8,10},{10,12},{12... | collective-permute-start | bytes 2359304 | tf_op jit(solution)/shard_map/ppermute | solution.py:77
  92.9 18.3 %collective-permute-start.5 = (bf16[256,1536]{1,0:T(8,128)(2,1)}, bf16[256,1536]{1,0:T(8,128)(2,1)S(1)}, u32[]{:S(2)}, u32[]{:S(2)}) collective-permute-start(bf16[256,1536]{1,0:T(8,128)(2,1)} %collective-permute-done.4), channel_id=1, source_target_pairs={{2,0},{4,2},{6,4},{7,6},{5,7},{3,5},{1,3},{0,1},{10,8},{12,10},{14... | collective-permute-start | bytes 2359304 | tf_op jit(solution)/shard_map/ppermute | solution.py:80
  178.7 18.3 %collective-permute-start.10 = (bf16[256,1536]{1,0:T(8,128)(2,1)S(1)}, bf16[256,1536]{1,0:T(8,128)(2,1)S(1)}, u32[]{:S(2)}, u32[]{:S(2)}) collective-permute-start(bf16[256,1536]{1,0:T(8,128)(2,1)S(1)} %add_convert_fusion.14), channel_id=1, source_target_pairs={{2,0},{4,2},{6,4},{7,6},{5,7},{3,5},{1,3},{0,1},{10,8},{12,10},{14... | collective-permute-start | bytes 2359304 | tf_op jit(solution)/shard_map/ppermute | solution.py:80
  216.6 23.5 %collective-permute-start.25 = (bf16[256,1536]{1,0:T(8,128)(2,1)S(1)}, bf16[256,1536]{1,0:T(8,128)(2,1)S(1)}, u32[]{:S(2)}, u32[]{:S(2)}) collective-permute-start(bf16[256,1536]{1,0:T(8,128)(2,1)S(1)} %get-tuple-element.70), channel_id=1, source_target_pairs={{2,0},{4,2},{6,4},{7,6},{5,7},{3,5},{1,3},{0,1},{10,8},{12,10},{14... | collective-permute-start | bytes 2359304 | tf_op jit(solution)/shard_map/ppermute | solution.py:80
  217.6 18.7 %collective-permute-start.21 = (bf16[256,1536]{1,0:T(8,128)(2,1)S(1)}, bf16[256,1536]{1,0:T(8,128)(2,1)S(1)}, u32[]{:S(2)}, u32[]{:S(2)}) collective-permute-start(bf16[256,1536]{1,0:T(8,128)(2,1)S(1)} %get-tuple-element.70), channel_id=1, source_target_pairs={{0,2},{2,4},{4,6},{6,7},{7,5},{5,3},{3,1},{1,0},{8,10},{10,12},{12... | collective-permute-start | bytes 2359304 | tf_op jit(solution)/shard_map/ppermute | solution.py:77
  237.1 18.5 %collective-permute-start.22 = (bf16[256,1536]{1,0:T(8,128)(2,1)S(1)}, bf16[256,1536]{1,0:T(8,128)(2,1)S(1)}, u32[]{:S(2)}, u32[]{:S(2)}) collective-permute-start(bf16[256,1536]{1,0:T(8,128)(2,1)S(1)} %collective-permute-done.21), channel_id=1, source_target_pairs={{0,2},{2,4},{4,6},{6,7},{7,5},{5,3},{3,1},{1,0},{8,10},{10,12},{12... | collective-permute-start | bytes 2359304 | tf_op jit(solution)/shard_map/ppermute | solution.py:77
  240.1 20.4 %collective-permute-start.26 = (bf16[256,1536]{1,0:T(8,128)(2,1)S(1)}, bf16[256,1536]{1,0:T(8,128)(2,1)S(1)}, u32[]{:S(2)}, u32[]{:S(2)}) collective-permute-start(bf16[256,1536]{1,0:T(8,128)(2,1)S(1)} %collective-permute-done.25), channel_id=1, source_target_pairs={{2,0},{4,2},{6,4},{7,6},{5,7},{3,5},{1,3},{0,1},{10,8},{12,10},{14... | collective-permute-start | bytes 2359304 | tf_op jit(solution)/shard_map/ppermute | solution.py:80
  287.6 53.0 %all-to-all-start.1 = ((f32[8,1,256]{2,1,0:T(1,128)}), f32[8,1,256]{2,1,0:T(1,128)S(1)}, u32[]{:S(2)}, u32[]{:S(2)}) async-start(f32[8,1,256]{2,1,0:T(1,128)} %copy.129), calls=%async_computation.1 | async-start | bytes 16384 | tf_op jit(solution)/shard_map/all_to_all | solution.py:194
  308.5 43.4 %collective-permute-start.75 = (bf16[2,1,192,1536]{3,2,1,0:T(8,128)(2,1)}, bf16[2,1,192,1536]{3,2,1,0:T(8,128)(2,1)}, u32[]{:S(2)}, u32[]{:S(2)}) collective-permute-start(bf16[2,1,192,1536]{3,2,1,0:T(8,128)(2,1)} %constant_dynamic-slice_fusion.1), channel_id=1, source_target_pairs={{0,8},{8,0},{1,9},{9,1},{2,10},{10,2},{3,11},{11,3},{4,12},{12,4},... | collective-permute-start | bytes 3538952 | tf_op jit(solution)/shard_map/ppermute | solution.py:138
  327.6 27.6 %collective-permute-start.71 = (bf16[2,1,384,768]{3,2,1,0:T(8,128)(2,1)}, bf16[2,1,384,768]{3,2,1,0:T(8,128)(2,1)}, u32[]{:S(2)}, u32[]{:S(2)}) collective-permute-start(bf16[2,1,384,768]{3,2,1,0:T(8,128)(2,1)} %constant_dynamic-slice_fusion.5), channel_id=1, source_target_pairs={{0,8},{8,0},{1,9},{9,1},{2,10},{10,2},{3,11},{11,3},{4,12},{12,4},... | collective-permute-start | bytes 3538952 | tf_op jit(solution)/shard_map/ppermute | solution.py:138
  327.6 42.9 %collective-permute-start.73 = (bf16[2,1,384,768]{3,2,1,0:T(8,128)(2,1)}, bf16[2,1,384,768]{3,2,1,0:T(8,128)(2,1)}, u32[]{:S(2)}, u32[]{:S(2)}) collective-permute-start(bf16[2,1,384,768]{3,2,1,0:T(8,128)(2,1)} %constant_dynamic-slice_fusion.3), channel_id=1, source_target_pairs={{0,8},{8,0},{1,9},{9,1},{2,10},{10,2},{3,11},{11,3},{4,12},{12,4},... | collective-permute-start | bytes 3538952 | tf_op jit(solution)/shard_map/ppermute | solution.py:138
  348.4 18.7 %collective-permute-start.34 = (bf16[256,1536]{1,0:T(8,128)(2,1)S(1)}, bf16[256,1536]{1,0:T(8,128)(2,1)S(1)}, u32[]{:S(2)}, u32[]{:S(2)}) collective-permute-start(bf16[256,1536]{1,0:T(8,128)(2,1)S(1)} %pad_maximum_fusion.4), channel_id=1, source_target_pairs={{0,2},{2,4},{4,6},{6,7},{7,5},{5,3},{3,1},{1,0},{8,10},{10,12},{12... | collective-permute-start | bytes 2359304 | tf_op jit(solution)/shard_map/ppermute | solution.py:77
  353.6 38.4 %collective-permute-start.76 = (bf16[1,1,192,1536]{3,2,1,0:T(8,128)(2,1)S(1)}, bf16[1,1,192,1536]{3,2,1,0:T(8,128)(2,1)S(1)}, u32[]{:S(2)}, u32[]{:S(2)}) collective-permute-start(bf16[1,1,192,1536]{3,2,1,0:T(8,128)(2,1)S(1)} %constant_dynamic-slice_fusion), channel_id=1, source_target_pairs={{0,16},{16,0},{1,17},{17,1},{2,18},{18,2},{3,19},{19,3},{4,20},{20... | collective-permute-start | bytes 1769480 | tf_op jit(solution)/shard_map/ppermute | solution.py:138
  356.8 34.1 %collective-permute-start.72 = (bf16[1,1,384,768]{3,2,1,0:T(8,128)(2,1)S(1)}, bf16[1,1,384,768]{3,2,1,0:T(8,128)(2,1)S(1)}, u32[]{:S(2)}, u32[]{:S(2)}) collective-permute-start(bf16[1,1,384,768]{3,2,1,0:T(8,128)(2,1)S(1)} %constant_dynamic-slice_fusion.4), channel_id=1, source_target_pairs={{0,16},{16,0},{1,17},{17,1},{2,18},{18,2},{3,19},{19,3},{4,20},{20... | collective-permute-start | bytes 1769480 | tf_op jit(solution)/shard_map/ppermute | solution.py:138
  389.3 47.6 %collective-permute-start.74 = (bf16[1,1,384,768]{3,2,1,0:T(8,128)(2,1)}, bf16[1,1,384,768]{3,2,1,0:T(8,128)(2,1)}, u32[]{:S(2)}, u32[]{:S(2)}) collective-permute-start(bf16[1,1,384,768]{3,2,1,0:T(8,128)(2,1)} %constant_dynamic-slice_fusion.2), channel_id=1, source_target_pairs={{0,16},{16,0},{1,17},{17,1},{2,18},{18,2},{3,19},{19,3},{4,20},{20... | collective-permute-start | bytes 1769480 | tf_op jit(solution)/shard_map/ppermute | solution.py:138
  423.8 23.0 %collective-permute-start.59 = (bf16[8,1,96,1536]{3,2,1,0:T(8,128)(2,1)S(1)}, bf16[8,1,96,1536]{3,2,1,0:T(8,128)(2,1)S(1)}, u32[]{:S(2)}, u32[]{:S(2)}) collective-permute-start(bf16[8,1,96,1536]{3,2,1,0:T(8,128)(2,1)S(1)} %constant_dynamic-slice_fusion.7), channel_id=1, source_target_pairs={{0,8},{8,0},{1,9},{9,1},{2,10},{10,2},{3,11},{11,3},{4,12},{12,4},... | collective-permute-start | bytes 7077896 | tf_op jit(solution)/shard_map/ppermute | solution.py:138
  429.5 25.5 %collective-permute-start.47 = (bf16[8,1,96,2048]{3,2,1,0:T(8,128)(2,1)S(1)}, bf16[8,1,96,2048]{3,2,1,0:T(8,128)(2,1)S(1)}, u32[]{:S(2)}, u32[]{:S(2)}) collective-permute-start(bf16[8,1,96,2048]{3,2,1,0:T(8,128)(2,1)S(1)} %constant_dynamic-slice_fusion.9), channel_id=1, source_target_pairs={{0,8},{8,0},{1,9},{9,1},{2,10},{10,2},{3,11},{11,3},{4,12},{12,4},... | collective-permute-start | bytes 9437192 | tf_op jit(solution)/shard_map/ppermute | solution.py:138
  447.6 29.0 %collective-permute-start.60 = (bf16[8,1,48,1536]{3,2,1,0:T(8,128)(2,1)S(1)}, bf16[8,1,48,1536]{3,2,1,0:T(8,128)(2,1)S(1)}, u32[]{:S(2)}, u32[]{:S(2)}) collective-permute-start(bf16[8,1,48,1536]{3,2,1,0:T(8,128)(2,1)S(1)} %constant_dynamic-slice_fusion.6), channel_id=1, source_target_pairs={{0,16},{16,0},{1,17},{17,1},{2,18},{18,2},{3,19},{19,3},{4,20},{20... | collective-permute-start | bytes 3538952 | tf_op jit(solution)/shard_map/ppermute | solution.py:138
  457.9 49.8 %collective-permute-start.48 = (bf16[8,1,48,2048]{3,2,1,0:T(8,128)(2,1)}, bf16[8,1,48,2048]{3,2,1,0:T(8,128)(2,1)}, u32[]{:S(2)}, u32[]{:S(2)}) collective-permute-start(bf16[8,1,48,2048]{3,2,1,0:T(8,128)(2,1)} %constant_dynamic-slice_fusion.8), channel_id=1, source_target_pairs={{0,16},{16,0},{1,17},{17,1},{2,18},{18,2},{3,19},{19,3},{4,20},{20... | collective-permute-start | bytes 4718600 | tf_op jit(solution)/shard_map/ppermute | solution.py:138
  485.1 27.2 %collective-permute-start.66 = (bf16[48,1536]{1,0:T(8,128)(2,1)S(1)}, bf16[48,1536]{1,0:T(8,128)(2,1)S(1)}, u32[]{:S(2)}, u32[]{:S(2)}) collective-permute-start(bf16[48,1536]{1,0:T(8,128)(2,1)S(1)} %pad_maximum_fusion.11), channel_id=1, source_target_pairs={{0,2},{2,4},{4,6},{6,7},{7,5},{5,3},{3,1},{1,0},{8,10},{10,12},{12... | collective-permute-start | bytes 442376 | tf_op jit(solution)/shard_map/ppermute | solution.py:77
  485.7 26.6 %collective-permute-start.62 = (bf16[48,1536]{1,0:T(8,128)(2,1)S(1)}, bf16[48,1536]{1,0:T(8,128)(2,1)S(1)}, u32[]{:S(2)}, u32[]{:S(2)}) collective-permute-start(bf16[48,1536]{1,0:T(8,128)(2,1)S(1)} %pad_maximum_fusion.10), channel_id=1, source_target_pairs={{2,0},{4,2},{6,4},{7,6},{5,7},{3,5},{1,3},{0,1},{10,8},{12,10},{14... | collective-permute-start | bytes 442376 | tf_op jit(solution)/shard_map/ppermute | solution.py:80
  (196 other events, 1719.7 us)

commit v2 on v1

v2 whole, which is shorter than its diff:
```python
import functools
import math

import jax
import jax.numpy as jnp
import numpy as np
from jax import lax
from jax.experimental import pallas as pl
from jax.experimental.pallas import tpu as pltpu
from jax.sharding import Mesh
from jax.sharding import PartitionSpec as P

H = 12
KVH = 2
HEAD = 128

EPSILON = 1e-06
ROPE_BASE = 10000.0
NEG_FILL = -1e30
ALL = ("x", "c", "z", "y")
EP = ("z", "y")
F32 = jnp.float32
BF16 = jnp.bfloat16
RING_LIMIT = 16


def dot(a, b, dims=((1,), (0,))):
    return lax.dot_general(a, b, (dims, ((), ())), preferred_element_type=F32)


def dot_nt(a, b):
    return dot(a, b, ((1,), (1,)))


def dot_tn(a, b):
    return dot(a, b, ((0,), (0,)))


def activate(gate_pre, up_pre):
    return jax.nn.gelu(gate_pre, approximate=True) * up_pre


class Ring:
    def __init__(self, z_size, y_size):
        cycle = [(z, 0) for z in range(z_size)]
        for step, z in enumerate(reversed(range(z_size))):
            rest = list(range(1, y_size))
            cycle += [(z, y) for y in (rest if step % 2 == 0 else rest[::-1])]
        self.order = [z * y_size + y for z, y in cycle]
        self.size = len(self.order)
        self.half = self.size // 2
        n = self.size
        self.forward = [(self.order[i], self.order[(i + 1) % n]) for i in range(n)]
        self.backward = [(b, a) for a, b in self.forward]
        self.place = [self.order.index(e) for e in range(n)]

    def fwd(self, a):
        return lax.ppermute(a, EP, self.forward)

    def bwd(self, a):
        return lax.ppermute(a, EP, self.backward)

    def owners(self):
        mine = jnp.asarray(self.place, jnp.int32)[lax.axis_index(EP)]
        behind = (mine - jnp.arange(self.size, dtype=jnp.int32)) % self.size
        return jnp.asarray(self.order, jnp.int32)[behind]

    def pair(self, s):
        return sorted({s, (self.size - s) % self.size})

    def gather(self, a, cut, use, lag, beside=lambda step, sent: ()):
        ahead = behind = a
        ready = {0: a}
        open_steps = [0]
        for s in range(1, self.half + 1):
            sent = (ahead, behind)
            if s < self.half:
                ahead, behind = self.fwd(ahead), self.bwd(behind)
            else:
                ahead, behind = self.fwd(ahead[:cut]), self.bwd(behind[cut:])
            made = [beside(s - 1, sent)]
            while open_steps and open_steps[0] + lag <= s - 1:
                step = open_steps.pop(0)
                made.append(use({j: [after(ready[j], sent) if lag else ready[j]] for j in self.pair(step)}))
            ahead, behind, _ = lax.optimization_barrier((ahead, behind, made))
            if s < self.half:
                ready[s], ready[self.size - s] = ahead, behind
                open_steps.append(s)
        made = use({self.half: [ahead, behind]})
        for step in reversed(open_steps):
            use({j: [after(ready[j], made)] for j in self.pair(step)})

    def scatter_sum(self, terms, cut, beside=lambda step, sent: ()):
        def add(a, b):
            return (a.astype(F32) + b.astype(F32)).astype(BF16)

        far = terms(self.half)
        down, up = far[:cut], far[cut:]
        for s in range(self.half, 0, -1):
            sent = (down, up)
            down, up = self.bwd(down), self.fwd(up)
            down, up, _ = lax.optimization_barrier((down, up, beside(self.half - s, sent)))
            if s == self.half:
                near, away = terms(s - 1), terms(s + 1)
                down = jnp.concatenate([add(near[:cut], down), near[cut:]], axis=0)
                up = jnp.concatenate([away[:cut], add(away[cut:], up)], axis=0)
            elif s > 1:
                down, up = add(down, terms(s - 1)), add(up, terms(self.size - s + 1))
        return down, up, terms(0)


def butterfly_sum(a, axes):
    for axis in axes:
        size = lax.axis_size(axis)
        step = 1
        while step < size:
            a = a + lax.ppermute(a, axis, [(i, i ^ step) for i in range(size)])
            step *= 2
    return a


class Sum:
    def __init__(self, a):
        self.a = a

    @staticmethod
    def send(a, axis, dim):
        size = lax.axis_size(axis)
        if size != 2:
            got = lax.psum_scatter(a, axis, scatter_dimension=dim, tiled=True)
            return jnp.zeros_like(got), got
        me = lax.axis_index(axis)
        mine = lax.dynamic_slice_in_dim(a, me, 1, dim)
        other = lax.dynamic_slice_in_dim(a, 1 - me, 1, dim)
        return mine, lax.ppermute(other, axis, [(0, 1), (1, 0)])

    def over_cores(self, tie):
        self.mine, self.got = self.send(after(self.a, tie), "c", 1)

    def over_x(self, tie):
        mine, got = self.mine, after(self.got, tie)
        both = (mine.astype(F32) + got.astype(F32)).astype(BF16)
        self.mine, self.got = self.send(both, "x", 0)
        return both

    def result(self, tie):
        got = after(self.got, tie)
        return self.mine.astype(F32) + got.astype(F32)


class RingExperts:
    def __init__(self, ring, block, gates, top, w_gate, w_up, w_down):
        self.ring, self.block = ring, block
        self.experts, self.rows = gates.shape
        self.weights = (w_gate, w_up, w_down)
        self.cut = self.rows // 2
        self.expert = lax.axis_index(EP).reshape(1)

    def forward(self, gather_beside, beside):
        self.rows_in, self.saved = {}, {}
        terms, counts = {}, {}

        def use(blocks):
            made = expert_forward(list(blocks.values()), self.experts, self.expert, *self.weights)
            for j, (rows, term, gate_pre, up_pre, hidden, weight, count) in zip(blocks, made):
                self.rows_in[j], terms[j], counts[j] = rows, term, count
                self.saved[j] = (gate_pre, up_pre, hidden, weight)
            return made

        self.ring.gather(self.block, self.cut, use, 1, gather_beside)
        count = sum(counts[j] for j in range(self.ring.size))[0, 0]
        return self.ring.scatter_sum(terms.get, self.cut, beside), count

    def backward(self, grad_out):
        grads_in, gate_lows, up_lows, scaled, terms = {}, {}, {}, {}, {}

        def use(blocks):
            saved = [self.saved[j] for j in blocks]
            made = expert_backward(list(blocks.values()), saved, self.experts, self.expert, *self.weights)
            for j, each in zip(blocks, made):
                grads_in[j], terms[j], gate_lows[j], up_lows[j], scaled[j] = each
            return made

        self.ring.gather(grad_out.astype(BF16), self.cut, use, 0)
        sums = []

        def joined(parts):
            return jnp.concatenate([parts[j] for j in range(self.ring.size)], axis=0)

        def beside(step, sent):
            made = []
            if step == 0:
                self.joined = after(joined(self.rows_in), sent)
                sums.append(expert_sum(self.joined, joined(after(gate_lows, sent))))
                made.append(sums[0].a)
            if step == 1:
                sums[0].over_cores(sent)
                sums.append(expert_sum(self.joined, joined(after(up_lows, sent))))
                made.append(sums[1].a)
            if step == 2:
                made.append(sums[0].over_x(sent))
                sums[1].over_cores(sent)
                sums.append(expert_sum(joined(after(scaled, sent)), joined(after(grads_in, sent))))
                made.append(sums[2].a)
            if step == 3:
                made.append(sums[1].over_x(sent))
                made.append(sums[0].got)
                sums[2].over_cores(sent)
            return made

        return self.ring.scatter_sum(terms.get, self.cut, beside), sums


def expert_sum(a, b):
    product = dot_tn(a, b).astype(BF16)
    return Sum(product.reshape(lax.axis_size("x"), lax.axis_size("c"), -1, product.shape[1]))


class SlotExperts:
    def __init__(self, ring, block, gates, top, w_gate, w_up, w_down):
        experts, rows = gates.shape
        moe_in, route_hot = block[:rows], gates.T > 0
        self.count_here = jnp.full((8, 128), block[rows, -1].astype(F32))
        self.slots = 3 * rows * top // (2 * experts)
        self.group = ring.size
        self.moe_in, self.weights = moe_in, (w_gate, w_up, w_down)
        places = jnp.arange(rows)
        earlier = (places[:, None] > places[None, :]).astype(BF16)
        rank = dot(earlier, route_hot.astype(BF16)).T[:, None, :]
        slot = jnp.arange(self.slots, dtype=F32)[None, :, None]
        picks = ((rank == slot) & route_hot.T[:, None, :]).reshape(experts * self.slots, rows)
        self.picks = picks.astype(BF16)
        self.slot_gate = jnp.where(picks, jnp.repeat(gates, self.slots, axis=0), 0.0)

    def swap(self, rows):
        blocks = rows.reshape(self.group, -1, rows.shape[1])
        return lax.all_to_all(blocks, EP, 0, 0, tiled=True).reshape(rows.shape)

    def forward(self, gather_beside, beside):
        w_gate, w_up, w_down = self.weights
        self.arrived = self.swap(dot(self.picks, self.moe_in).astype(BF16))
        self.gate_pre = dot(self.arrived, w_gate)
        self.up_pre = dot(self.arrived, w_up)
        self.hidden = activate(self.gate_pre, self.up_pre).astype(BF16)
        self.returned = self.swap(dot(self.hidden, w_down).astype(BF16))
        count = butterfly_sum(self.count_here, ("y", "z"))[0, 0]
        return (jnp.dot(self.slot_gate.T, self.returned.astype(F32), precision=lax.Precision.HIGHEST),), count

    def backward(self, grad_out):
        w_gate, w_up, w_down = self.weights
        grad_low = grad_out.astype(BF16)
        rows, experts = grad_out.shape[0], self.picks.shape[0] // self.slots
        products = dot_nt(grad_low, self.returned) * self.picks.T.astype(F32)
        grad_gates = jnp.sum(products.reshape(rows, experts, self.slots), axis=2)
        slot_gate = jnp.sum(self.slot_gate, axis=1, keepdims=True)
        grads_in = self.swap((dot(self.picks, grad_low) * slot_gate).astype(BF16))
        _, pull = jax.vjp(activate, self.gate_pre, self.up_pre)
        grad_gate, grad_up = pull(dot_nt(grads_in, w_down))
        gate_low, up_low = grad_gate.astype(BF16), grad_up.astype(BF16)
        back = self.swap((dot_nt(gate_low, w_gate) + dot_nt(up_low, w_up)).astype(BF16))
        sums = [
            expert_sum(self.arrived, gate_low),
            expert_sum(self.arrived, up_low),
            expert_sum(self.hidden, grads_in),
        ]
        for each in sums:
            each.over_cores(each.a)
        for each in sums[:2]:
            each.over_x(each.a)
        notes = jnp.pad(grad_gates.T, ((0, 0), (0, grad_out.shape[1] - rows)))
        return (jnp.concatenate([dot_tn(self.picks, back), notes], axis=0),), sums


def rope_tables(length):
    half = HEAD // 2
    frequency = ROPE_BASE ** (-np.arange(half, dtype=np.float64) / half)
    angles = np.arange(length, dtype=np.float64)[:, None] * frequency[None, :]
    cosine, sine = np.cos(angles), np.sin(angles)
    pairs = np.concatenate([cosine, cosine], axis=1), np.concatenate([-sine, sine], axis=1)
    return tuple(jnp.asarray(p, F32) for p in pairs)


def turned(values, cosine, sine):
    return values * cosine + pltpu.roll(values, HEAD // 2, 1) * sine


def on_chip(count):
    return [pl.BlockSpec(memory_space=pltpu.VMEM)] * count


def in_place(count):
    return [pl.BlockSpec(memory_space=pltpu.HBM)] * count


def fetch(sources, buffers, semaphores):
    copies = [pltpu.make_async_copy(s, b, semaphores.at[i]) for i, (s, b) in enumerate(zip(sources, buffers))]
    for copy in copies:
        copy.start()
    return copies


def call(body, ins, places, outs, scratch=(), flops=0, moved=0, out_places=None, limit=28):
    return pl.pallas_call(
        body,
        out_shape=[jax.ShapeDtypeStruct(s, d) for s, d in outs],
        in_specs=places,
        out_specs=out_places or on_chip(len(outs)),
        scratch_shapes=list(scratch),
        compiler_params=pltpu.CompilerParams(vmem_limit_bytes=limit << 20),
        cost_estimate=pl.CostEstimate(flops=int(flops), bytes_accessed=int(moved), transcendentals=0),
    )(*ins)


def gelu_parts(values):
    c = math.sqrt(2.0 / math.pi)
    square = values * values
    level = 0.5 + 0.5 * jnp.tanh(c * values * (1.0 + 0.044715 * square))
    slope = level + 2.0 * c * values * level * (1.0 - level) * (1.0 + 3 * 0.044715 * square)
    return level, slope


def note_rows(experts, expert, columns):
    rows = lax.broadcasted_iota(jnp.int32, (experts, columns), 0)
    return (rows == expert).astype(F32)


def expert_forward_body(parts, experts, *refs):
    expert, w_gate, w_up, w_down = refs[0][0], *refs[1:4]
    at = 4
    inputs = []
    for count in parts:
        inputs.append(refs[at : at + count])
        at += count
    mine = note_rows(experts, expert, 128).astype(BF16)
    for pieces in inputs:
        rows_o, term_o, gate_o, up_o, hidden_o, weight_o, count_o = refs[at : at + 7]
        at += 7
        block = jnp.concatenate([p[...] for p in pieces], axis=0)
        rows = block.shape[0] - experts
        notes = block[rows:]
        block = block[:rows]
        rows_o[...] = block
        weight = dot_tn(notes[:, :rows], mine) + dot_tn(notes[:, rows : 2 * rows], mine)
        weight_o[...] = weight
        count_o[...] = notes[:, notes.shape[1] - 128 :].astype(F32)
        step = 256
        for f in range(0, w_gate.shape[1], step):
            gate_pre = dot(block, w_gate[:, f : f + step])
            up_pre = dot(block, w_up[:, f : f + step])
            level, _ = gelu_parts(gate_pre)
            hidden_o[:, f : f + step] = (gate_pre * level * up_pre).astype(BF16)
            gate_o[:, f : f + step] = gate_pre.astype(BF16)
            up_o[:, f : f + step] = up_pre.astype(BF16)
        hidden = hidden_o[...]
        wide = jnp.concatenate([weight] * (step // 128), axis=1)
        for c in range(0, block.shape[1], step):
            term_o[:, c : c + step] = (dot(hidden, w_down[:, c : c + step]) * wide).astype(BF16)


def expert_forward(blocks, experts, expert, w_gate, w_up, w_down):
    parts = [len(pieces) for pieces in blocks]
    flat = [p for pieces in blocks for p in pieces]
    rows = sum(p.shape[0] for p in blocks[0]) - experts
    width, inner = w_gate.shape
    one = [((rows, width), BF16)] * 2 + [((rows, inner), BF16)] * 3 + [((rows, 128), F32), ((experts, 128), F32)]
    made = call(
        functools.partial(expert_forward_body, parts, experts),
        (expert, w_gate, w_up, w_down, *flat),
        [pl.BlockSpec(memory_space=pltpu.SMEM)] + on_chip(3 + len(flat)),
        one * len(blocks),
        flops=len(blocks) * 6 * rows * width * inner,
        limit=24,
    )
    return [made[7 * i : 7 * i + 7] for i in range(len(blocks))]


def expert_backward_body(parts, experts, *refs):
    expert, w_gate, w_up, w_down = refs[0][0], *refs[1:4]
    at = 4
    inputs = []
    for count in parts:
        inputs.append((refs[at : at + count], *refs[at + count : at + count + 4]))
        at += count + 4
    for pieces, gate_ref, up_ref, hidden_ref, weight_ref in inputs:
        grads_o, term_o, gate_o, up_o, scaled_o = refs[at : at + 5]
        at += 5
        grads = jnp.concatenate([p[...] for p in pieces], axis=0)
        grads_o[...] = grads
        rows, width = grads.shape
        step = 256
        ones = jnp.ones((8, step), BF16)
        wide = jnp.concatenate([weight_ref[...]] * (step // 128), axis=1)
        sums = jnp.zeros((8, rows), F32)
        for f in range(0, w_down.shape[0], step):
            raw = dot_nt(grads, w_down[f : f + step, :])
            hidden = hidden_ref[:, f : f + step].astype(F32)
            product = raw * hidden
            high = product.astype(BF16)
            sums = sums + dot_nt(ones, high) + dot_nt(ones, (product - high.astype(F32)).astype(BF16))
            scaled_o[:, f : f + step] = (hidden * wide).astype(BF16)
            gate_pre = gate_ref[:, f : f + step].astype(F32)
            level, slope = gelu_parts(gate_pre)
            grad_hidden = raw * wide
            gate_o[:, f : f + step] = (grad_hidden * up_ref[:, f : f + step].astype(F32) * slope).astype(BF16)
            up_o[:, f : f + step] = (grad_hidden * gate_pre * level).astype(BF16)
        high = sums.astype(BF16).astype(F32)
        notes = jnp.concatenate([high, sums - high, jnp.zeros((8, width - 2 * rows), F32)], axis=1)
        mine = note_rows(experts, expert, width)
        notes = (jnp.broadcast_to(notes[:1], (experts, width)) * mine).astype(BF16)
        gate_low, up_low = gate_o[...], up_o[...]
        terms = [
            (dot_nt(gate_low, w_gate[c : c + step, :]) + dot_nt(up_low, w_up[c : c + step, :])).astype(BF16)
            for c in range(0, width, step)
        ]
        term_o[...] = jnp.concatenate([jnp.concatenate(terms, axis=1), notes], axis=0)


def expert_backward(blocks, saved, experts, expert, w_gate, w_up, w_down):
    parts = [len(pieces) for pieces in blocks]
    flat = [p for pieces, kept in zip(blocks, saved) for p in (*pieces, *kept)]
    rows, inner = saved[0][0].shape
    width = w_gate.shape[0]
    one = [((rows, width), BF16), ((rows + experts, width), BF16)] + [((rows, inner), BF16)] * 3
    made = call(
        functools.partial(expert_backward_body, parts, experts),
        (expert, w_gate, w_up, w_down, *flat),
        [pl.BlockSpec(memory_space=pltpu.SMEM)] + on_chip(3 + len(flat)),
        one * len(blocks),
        flops=len(blocks) * 6 * rows * width * inner,
        limit=24,
    )
    return [made[5 * i : 5 * i + 5] for i in range(len(blocks))]


def attention_forward_body(*refs):
    hbm, outs_hbm, (block_o, gates_o), refs = refs[:13], refs[13:20], refs[20:22], refs[22:]
    bufs, stores, sems, out_sems = refs[:13], refs[13:20], refs[20], refs[21]
    copies = fetch(hbm, bufs, sems)
    tokens, segments, routes, valid, gain_one, gain_two, cosine, sine, router = bufs[:9]
    w_key, w_value, w_query, w_out = bufs[9:]
    normed_o, query_o, key_o, value_o, weights_o, context_o, mixed_o = stores
    leaving = []

    def leave(*which):
        for i in which:
            leaving.append(pltpu.make_async_copy(stores[i], outs_hbm[i], out_sems.at[i]))
            leaving[-1].start()

    for copy in copies[:9]:
        copy.wait()
    copies = copies[9:]
    rows, width = tokens.shape
    groups = H // KVH
    rows_in = tokens[...].astype(F32)
    inverse = lax.rsqrt(jnp.mean(rows_in * rows_in, axis=1, keepdims=True) + EPSILON)
    normed = (rows_in * inverse * gain_one[...].astype(F32)).astype(BF16)
    normed_o[...] = normed
    leave(0)
    cos, sin = cosine[...], sine[...]
    copies[0].wait()
    keys = dot(normed, w_key[...])
    for g in range(KVH):
        at = pl.ds(g * HEAD, HEAD)
        key_o[:, at] = turned(keys[:, g * HEAD : (g + 1) * HEAD], cos, sin).astype(BF16)
    copies[1].wait()
    value_o[...] = dot(normed, w_value[...]).astype(BF16)
    leave(2, 3)
    copies[2].wait()
    half = rows // 2
    lower = lax.broadcasted_iota(jnp.int32, (rows, rows), 0) >= lax.broadcasted_iota(jnp.int32, (rows, rows), 1)
    across = jnp.broadcast_to(segments[...].astype(F32), (rows, rows))
    allowed = (across == across.T) & lower
    for g in range(KVH):
        span = groups * HEAD
        queries = dot(normed, w_query[:, g * span : (g + 1) * span])
        key = key_o[:, g * HEAD : (g + 1) * HEAD]
        value = value_o[:, g * HEAD : (g + 1) * HEAD]
        for i in range(groups):
            h = g * groups + i
            at = pl.ds(h * HEAD, HEAD)
            query = turned(queries[:, i * HEAD : (i + 1) * HEAD], cos, sin).astype(BF16)
            query_o[:, at] = query
            for first, last in ((0, half), (half, rows)):
                scores = dot_nt(query[first:last], key[:last]) * HEAD ** (-0.5)
                scores = jnp.where(allowed[first:last, :last], scores, NEG_FILL)
                peak = jnp.max(scores, axis=1, keepdims=True)
                terms = jnp.exp(scores - peak)
                weights = (terms / jnp.sum(terms, axis=1, keepdims=True)).astype(BF16)
                weights_o[h * rows + first : h * rows + last, :last] = weights
                context_o[first:last, at] = dot(weights, value[:last]).astype(BF16)
            weights_o[h * rows : h * rows + half, half:] = jnp.zeros((half, rows - half), BF16)
    leave(1, 4, 5)
    copies[3].wait()
    step = width // 3
    for c in range(0, width, step):
        mixed_o[:, c : c + step] = tokens[:, c : c + step].astype(F32) + dot(context_o[...], w_out[:, c : c + step])
    leave(6)
    mixed = mixed_o[...]
    inverse = lax.rsqrt(jnp.mean(mixed * mixed, axis=1, keepdims=True) + EPSILON)
    moe_in = (mixed * inverse * gain_two[...].astype(F32)).astype(BF16)
    experts = router.shape[0]
    logits = dot_nt(router[...], moe_in)
    ids = lax.broadcasted_iota(jnp.int32, (experts, rows), 0)
    hot = ids == routes[0:1, :]
    for k in range(1, routes.shape[0]):
        hot = hot | (ids == routes[k : k + 1, :])
    peak = jnp.max(jnp.where(hot, logits, NEG_FILL), axis=0, keepdims=True)
    terms = jnp.where(hot, jnp.exp(jnp.where(hot, logits - peak, 0.0)), 0.0)
    gates = terms / jnp.sum(terms, axis=0, keepdims=True)
    gates_o[...] = gates
    high = gates.astype(BF16).astype(F32)
    low = gates - high
    count = jnp.sum(valid[...].astype(F32), axis=1, keepdims=True)
    counts = jnp.broadcast_to(count, (experts, width - 2 * rows))
    notes = jnp.concatenate([high, low, counts], axis=1).astype(BF16)
    block_o[...] = jnp.concatenate([moe_in, notes], axis=0)
    for copy in leaving:
        copy.wait()


def attention_forward(tokens, segments, routes, valid, gain_one, gain_two, tables, router, weights):
    rows, width = tokens.shape
    experts = router.shape[1]
    w_query, w_key, w_value, w_out = weights
    ins = (tokens, segments, routes.T, valid, gain_one[None], gain_two[None], *tables, router.T)
    ins += (w_key, w_value, w_query, w_out)
    stores = [
        ((rows, width), BF16),
        ((rows, H * HEAD), BF16),
        ((rows, KVH * HEAD), BF16),
        ((rows, KVH * HEAD), BF16),
        ((H * rows, rows), BF16),
        ((rows, H * HEAD), BF16),
        ((rows, width), F32),
    ]
    return call(
        attention_forward_body,
        ins,
        in_place(len(ins)),
        stores + [((rows + experts, width), BF16), ((experts, rows), F32)],
        [pltpu.VMEM(a.shape, a.dtype) for a in ins]
        + [pltpu.VMEM(*store) for store in stores]
        + [pltpu.SemaphoreType.DMA((len(ins),)), pltpu.SemaphoreType.DMA((len(stores),))],
        flops=2 * rows * width * (2 * width + 4 * KVH * HEAD),
        moved=14 << 20,
        out_places=in_place(len(stores)) + on_chip(2),
        limit=60,
    )


def mixed_backward_body(parts, *refs):
    ins, outs = refs[:parts], refs[parts + 6 :]
    grad_out, mixed_ref, moe_in, gates, router, gain_two = refs[parts : parts + 6]
    branch_o, mixed_o, gain_o, router_o = outs
    rows, width = grad_out.shape
    experts = gates.shape[0]
    total = ins[0][...].astype(F32)
    for part in ins[1:]:
        total = total + part[...].astype(F32)
    notes = total[rows : rows + experts]
    grad_gates = notes[:, :rows] + notes[:, rows : 2 * rows]
    weights = gates[...]
    chosen = weights * (grad_gates - jnp.sum(weights * grad_gates, axis=0, keepdims=True))
    logits = chosen.astype(BF16)
    router_o[...] = dot(logits, moe_in[:rows])
    grad_in = total[:rows] + dot_tn(logits, router[...])
    mixed = mixed_ref[...]
    inverse = lax.rsqrt(jnp.mean(mixed * mixed, axis=1, keepdims=True) + EPSILON)
    normal = mixed * inverse
    gain_o[...] = jnp.sum(grad_in * normal, axis=0, keepdims=True)
    scaled = grad_in * gain_two[...].astype(F32)
    inner = jnp.mean(scaled * normal, axis=1, keepdims=True)
    grad_mixed = grad_out[...] + inverse * (scaled - normal * inner)
    mixed_o[...] = grad_mixed
    branch_o[...] = grad_mixed.astype(BF16)


def mixed_backward(parts, grad_out, mixed, block, gates, router, gain_two):
    rows, width = mixed.shape
    experts = router.shape[1]
    ins = (*parts, grad_out, mixed, block, gates, router.T, gain_two[None])
    outs = [((rows, width), BF16), ((rows, width), F32), ((1, width), F32), ((experts, width), F32)]
    return call(functools.partial(mixed_backward_body, len(parts)), ins, on_chip(len(ins)), outs, moved=9 << 20)


def attention_backward_body(branch, weights, query, key, value, cosine, sine, w_hbm, qkv_o, w_out, sems):
    rows = branch.shape[0]
    groups = H // KVH
    span = groups * HEAD
    copies = [
        pltpu.make_async_copy(w_hbm.at[pl.ds(g * span, span)], w_out.at[pl.ds(g * span, span)], sems.at[g])
        for g in range(KVH)
    ]
    for copy in copies:
        copy.start()
    cos, sin = cosine[...], -sine[...]
    half = rows // 2
    scale = HEAD ** (-0.5)
    for g in range(KVH):
        copies[g].wait()
        grad_context = dot_nt(branch[...], w_out[g * span : (g + 1) * span, :]).astype(BF16)
        k = key[:, g * HEAD : (g + 1) * HEAD]
        v = value[:, g * HEAD : (g + 1) * HEAD]
        grad_key = jnp.zeros((rows, HEAD), F32)
        grad_value = jnp.zeros((rows, HEAD), F32)
        for i in range(groups):
            h = g * groups + i
            q = query[:, h * HEAD : (h + 1) * HEAD]
            grad = grad_context[:, i * HEAD : (i + 1) * HEAD]
            low = weights[h * rows : (h + 1) * rows, :]
            grads = dot_nt(grad, v)
            full = low.astype(F32)
            product = full * grads
            scores = (product - full * jnp.sum(product, axis=1, keepdims=True)).astype(BF16)
            grad_query = dot(scores, k) * scale
            qkv_o[:, h * HEAD : (h + 1) * HEAD] = turned(grad_query, cos, sin).astype(BF16)
            grad_key = grad_key + dot_tn(scores, q)
            grad_value = grad_value + dot_tn(low, grad)
        at = (H + g) * HEAD
        qkv_o[:, at : at + HEAD] = turned(grad_key * scale, cos, sin).astype(BF16)
        at += KVH * HEAD
        qkv_o[:, at : at + HEAD] = grad_value.astype(BF16)


def attention_backward(branch, weights, query, key, value, tables, w_out):
    rows = branch.shape[0]
    ins = (branch, weights, query, key, value, *tables)
    outs = [((rows, (H + 2 * KVH) * HEAD), BF16)]
    scratch = [pltpu.VMEM(w_out.shape, BF16), pltpu.SemaphoreType.DMA((KVH,))]
    (made,) = call(
        attention_backward_body,
        ins + (w_out,),
        on_chip(len(ins)) + in_place(1),
        outs,
        scratch,
    )
    return made


def token_backward_body(qkv, tokens, grad_mixed, gain_one, *rest):
    hbm, (tokens_o, gain_o), bufs, sems = rest[:3], rest[3:5], rest[5:8], rest[8]
    copies = fetch(hbm, bufs, sems)
    rows_in = tokens[...].astype(F32)
    inverse = lax.rsqrt(jnp.mean(rows_in * rows_in, axis=1, keepdims=True) + EPSILON)
    normal = rows_in * inverse
    at = H * HEAD
    span = KVH * HEAD
    copies[0].wait()
    grads = dot_nt(qkv[:, at : at + span], bufs[0][...])
    copies[1].wait()
    grads = grads + dot_nt(qkv[:, at + span :], bufs[1][...])
    copies[2].wait()
    grads = grads + dot_nt(qkv[:, :at], bufs[2][...])
    gain_o[...] = jnp.sum(grads * normal, axis=0, keepdims=True)
    scaled = grads * gain_one[...].astype(F32)
    inner = jnp.mean(scaled * normal, axis=1, keepdims=True)
    tokens_o[...] = grad_mixed[...] + inverse * (scaled - normal * inner)


def token_backward(qkv, tokens, grad_mixed, gain_one, weights):
    rows, width = tokens.shape
    w_query, w_key, w_value, _ = weights
    hbm = (w_key, w_value, w_query)
    ins = (qkv, tokens, grad_mixed, gain_one[None])
    outs = [((rows, width), F32), ((1, width), F32)]
    return call(
        token_backward_body,
        ins + hbm,
        on_chip(len(ins)) + in_place(3),
        outs,
        [pltpu.VMEM(w.shape, BF16) for w in hbm] + [pltpu.SemaphoreType.DMA((3,))],
    )


def after(value, first):
    return lax.optimization_barrier((value, first))[0]


def rep_pairs(k):
    size = lax.axis_size(("x", "c"))
    return [(i, i ^ k) for i in range(size)]


def x_gather(a):
    size = lax.axis_size("x")
    return [a] + [lax.ppermute(a, "x", [(i, i ^ k) for i in range(size)]) for k in range(1, size)]


def core_gather(blocks):
    return [b for a in blocks for b in (a, lax.ppermute(a, "c", [(0, 1), (1, 0)]))]


def rep_gather(a):
    return core_gather(x_gather(a))


def rep_spread(a):
    size = lax.axis_size(("x", "c"))
    me = lax.axis_index(("x", "c"))
    share = a.shape[1] // size
    parts = []
    for k in range(size):
        part = lax.dynamic_slice_in_dim(a, (me ^ k) * share, share, 1)
        parts.append(lax.ppermute(part, ("x", "c"), rep_pairs(k)) if k else part)
    return jnp.concatenate(parts, axis=0)


def rep_columns(a):
    size = lax.axis_size(("x", "c"))
    stacked = jnp.stack(rep_gather(a))
    me = lax.axis_index(("x", "c"))
    return jnp.concatenate(
        [lax.dynamic_index_in_dim(stacked, me ^ i, 0, keepdims=False) for i in range(size)], axis=1
    )


def shards(
    ring,
    tokens,
    segments,
    routes,
    valid_mask,
    teacher,
    gain_one,
    w_query,
    w_key,
    w_value,
    w_out,
    gain_two,
    router,
    w_gate,
    w_up,
    w_down,
):
    length, width = tokens.shape
    experts_all = router.shape[1]
    tokens_all = length * lax.axis_size(ALL)
    w_gate, w_up, w_down = w_gate[0], w_up[0], w_down[0]
    valid_rows = valid_mask.reshape(length).astype(F32)
    tables = rope_tables(length)
    attn = (w_query, w_key, w_value, w_out)
    normed_low, query, key, value, weights_low, context, mixed_rows, block, gates = attention_forward(
        tokens, segments, routes, valid_mask, gain_one, gain_two, tables, router, attn
    )
    owners = ring.owners()
    form = RingExperts if ring.size <= RING_LIMIT else SlotExperts
    experts = form(ring, block, gates, routes.shape[1], w_gate, w_up, w_down)
    gathered = {}

    def beside(name, value):
        def work(step, sent):
            if step == 0:
                gathered[name] = x_gather(after(value, sent))
            if step == 2:
                gathered[name] = core_gather(after(gathered[name], sent))
            if step == 1 or step == 3:
                return gathered[name]
            return ()

        return work

    moe_parts, count_group = experts.forward(beside("normed", normed_low), beside("context", context))
    moe_out = sum(part.astype(F32) for part in moe_parts)
    if not gathered:
        gathered = {"normed": rep_gather(normed_low), "context": rep_gather(context)}
    count_total = butterfly_sum(jnp.full((8, 128), count_group), ("c", "x"))[0, 0]
    output_rows = mixed_rows + moe_out
    residual_gap = output_rows - teacher.astype(F32)
    numerator = jnp.sum(valid_rows * jnp.sum(residual_gap * residual_gap, axis=-1))
    grad_out = 2.0 * tokens_all / count_total * valid_rows[:, None] * residual_gap

    grad_out, gathered = lax.optimization_barrier((grad_out, gathered))
    normed_all = jnp.concatenate(gathered["normed"], axis=0)
    context_all = jnp.concatenate(gathered["context"], axis=0)
    back_parts, sums = experts.backward(grad_out)
    grad_branch, grad_mixed, grad_gain_two, grad_router = mixed_backward(
        back_parts, grad_out, mixed_rows, block, gates, router, gain_two
    )
    branch_spread = rep_spread(grad_branch)
    grad_qkv = attention_backward(grad_branch, weights_low, query, key, value, tables, w_out)
    qkv_spread = rep_spread(grad_qkv)
    grad_w_out = dot_tn(context_all, after(branch_spread, grad_qkv)).astype(BF16)
    grad_w_qkv = dot_tn(normed_all, after(qkv_spread, grad_w_out)).astype(BF16)
    grad_tokens, grad_gain_one = token_backward(
        after(grad_qkv, (grad_w_qkv, sums[1].got)), tokens, grad_mixed, gain_one, attn
    )
    sums[2].over_x(grad_w_qkv)

    def reduce_rows(g):
        part = g.astype(BF16).reshape(ring.size, -1, g.shape[1])
        cut = part.shape[1] // 2
        total = ring.scatter_sum(lambda j: lax.dynamic_index_in_dim(part, owners[j], 0, keepdims=False), cut)
        return rep_columns(sum(t.astype(F32) for t in total).astype(BF16)).astype(F32)

    shares = [each.result(grad_tokens)[0] for each in sums]
    out_share = reduce_rows(grad_w_out)
    qkv_share = reduce_rows(grad_w_qkv)
    small = jnp.concatenate(
        [grad_router.reshape(-1), grad_gain_two[0], grad_gain_one[0], jnp.full((128,), numerator)]
    ).reshape(-1, 128)
    flat = butterfly_sum(small, ("c", "x", "y", "z")).reshape(-1)
    at = width * experts_all
    return (
        output_rows.astype(BF16),
        flat[at + 2 * width] / count_total,
        grad_tokens,
        flat[at + width : at + 2 * width],
        qkv_share[:, : H * HEAD],
        qkv_share[:, H * HEAD : (H + KVH) * HEAD],
        qkv_share[:, (H + KVH) * HEAD :],
        out_share,
        flat[at : at + width],
        flat[:at].reshape(experts_all, width).T,
        shares[0],
        shares[1],
        shares[2],
    )


def solution(mesh):
    rep, ep = mesh.shape["rep"], mesh.shape["ep"]
    x_size = rep // 2
    y_size = x_size if ep % x_size == 0 else 1
    grid = Mesh(mesh.devices.reshape(x_size, 2, ep // y_size, y_size), ALL)
    rows = P(ALL, None)
    whole = P()
    expert = P(EP, None, None)
    return jax.shard_map(
        functools.partial(shards, Ring(ep // y_size, y_size)),
        mesh=grid,
        in_specs=(rows,) * 5 + (whole,) * 7 + (expert,) * 3,
        out_specs=(rows, whole, rows, whole)
        + (P(EP, None),) * 4
        + (whole, whole)
        + (P(EP, ("x", "c"), None),) * 3,
        check_vma=False,
    )
```

time: 562 us -> 426 us (0.76)
  matrix products: 120 us -> 28.4 us
  waiting for transfers between devices: 206 us -> 126 us
  Pallas kernels: 0 us -> 68.5 us
  starting transfers between devices: 91.3 us -> 74.3 us
  other arithmetic: 51.5 us -> 35 us
    dot_general x64 -> x5, matrix products: 112 us -> 28.4 us  [dot(): return lax.dot_general(a, b, (dims, ((), ())), preferred_element_type=F32)]
    pallas_call x0 -> x14, Pallas kernels: none -> 68.5 us  [call(): pl.pallas_call(body, out_shape=[jax.ShapeDtypeStruct(s, d) for s, d in ou...]
    ppermute x24, waiting for transfers between devices: 110 us -> 69.3 us  [fwd(): return lax.ppermute(a, EP, self.forward)]
    ppermute x24, waiting for transfers between devices: 45.7 us -> 16.1 us  [bwd(): return lax.ppermute(a, EP, self.backward)]
    unnamed x296 -> x319, local copies, waits for them, and re-layouts: 30.4 us -> 42.1 us
    ppermute x15 -> x7, starting transfers between devices: 20 us -> 8.23 us  [butterfly_sum(): a = a + lax.ppermute(a, axis, [(i, i ^ step) for i in range(size)])]
    all_to_all x2 -> x0, starting transfers between devices: 10 us -> none  [the longest x1 6.28 us: __init__(): gates = lax.all_to_all(gate_weights.T, EP, 0, 0, tiled=True)]
    dot_general x6 -> x0, matrix products: 8.46 us -> none  [the longest x1 2.94 us: shards(): jnp.einsum('kgqp,qkgc->pkc', attn_weights.astype(BF16), grad_context, pre...]
  transfers between devices with their start and end apart: 79 -> 79, of which waited for: 38 -> 34; matrix products, arithmetic and copies ran while one was open for 31% -> 22% of each run, Pallas kernels for 0% -> 12%
where the time goes in v2:
time: 426 us; the launch traced here: 418 us
  waiting for transfers between devices  126 us (30%)
  starting transfers between devices  74.3 us (17%)
  Pallas kernels  68.5 us (16%)
  local copies, waits for them, and re-layouts  63.8 us (15%)
  other arithmetic  35 us (8%)
  matrix products  28.4 us (7%)
  between operations  21.5 us (5%)
    ppermute x24, waiting for transfers between devices, fwd(): return lax.ppermute(a, EP, self.forward)  69.3 us
    pallas_call x14, Pallas kernels, call(): pl.pallas_call(body, out_shape=[jax.ShapeDtypeStruct(s, d) for s, d in ou...  68.5 us
    unnamed x319, local copies, waits for them, and re-layouts  42.1 us
    ppermute x24, starting transfers between devices, fwd(): return lax.ppermute(a, EP, self.forward)  34.8 us
    dot_general x5, matrix products, dot(): return lax.dot_general(a, b, (dims, ((), ())), preferred_element_type=F32)  28.4 us
    ppermute x24, starting transfers between devices, bwd(): return lax.ppermute(a, EP, self.backward)  19.3 us
    ppermute x24, waiting for transfers between devices, bwd(): return lax.ppermute(a, EP, self.backward)  16.1 us
    ppermute x4, waiting for transfers between devices, x_gather(): lax.ppermute(a, 'x', [(i, i ^ k) for i in range(size)])  14.9 us
  transfers between devices with their start and end apart: 79, of which 34 were waited for; matrix products, arithmetic and copies ran while one was open for 22% of the time, Pallas kernels for 12%

profile of v2, /device:TPU:0, one launch (start us, length us, event | category | flops | bytes accessed | tf_op | source)
XLA Modules:
  0.0 417.9 jit_solution(15153209964361288203)
XLA Ops:
  3.2 14.9 %shard_map.282 = (bf16[256,1536]{1,0:T(8,128)(2,1)}, bf16[256,1536]{1,0:T(8,128)(2,1)}, bf16[256,256]{1,0:T(8,128)(2,1)}, bf16[256,256]{1,0:T(8,128)(2,1)}, bf16...) custom-call(bf16[256,1536]{1,0:T(8,128)(2,1)} %tokens.1, ...), custom_call_target="tpu_custom_call" | custom-call | flops 3221225472 | bytes 14680064 | tf_op jit(solution)/shard_map/pallas_call | solution.py:303
  21.2 18.3 %collective-permute-done.refs_4_ = bf16[264,1536]{1,0:T(8,128)(2,1)} collective-permute-done((bf16[264,1536]{1,0:T(8,128)(2,1)}, bf16[264,1536]{1,0:T(8,128)(2,1)}, u32[]{:S(2)}, u32[]{:S(2)}) %collective-permute-start) | collective-permute-done | bytes 811040 | tf_op jit(solution)/shard_map/ppermute | solution.py:58
  55.0 5.9 %collective-permute-done.4 = bf16[256,1536]{1,0:T(8,128)(2,1)} collective-permute-done((bf16[256,1536]{1,0:T(8,128)(2,1)}, bf16[256,1536]{1,0:T(8,128)(2,1)}, u32[]{:S(2)}, u32[]{:S(2)}) %collective-permute-start.4) | collective-permute-done | bytes 786464 | tf_op jit(solution)/shard_map/ppermute | solution.py:686
  64.2 5.3 %shard_map.284 = (bf16[256,1536]{1,0:T(8,128)(2,1)S(1)}, bf16[256,1536]{1,0:T(8,128)(2,1)S(1)}, bf16[256,768]{1,0:T(8,128)(2,1)S(1)}, bf16[256,768]{1,0:T(8,128)...) custom-call(s32[1]{0:T(128)} %bitcast.2.refs_0_, ...), custom_call_target="tpu_custom_call" | custom-call | flops 3623878656 | tf_op jit(solution)/shard_map/pallas_call | solution.py:303
  83.3 5.3 %shard_map.285 = (bf16[256,1536]{1,0:T(8,128)(2,1)S(1)}, bf16[256,1536]{1,0:T(8,128)(2,1)S(1)}, bf16[256,768]{1,0:T(8,128)(2,1)S(1)}, bf16[256,768]{1,0:T(8,128)...) custom-call(s32[1]{0:T(128)} %bitcast.2.refs_0_, ...), custom_call_target="tpu_custom_call" | custom-call | flops 3623878656 | tf_op jit(solution)/shard_map/pallas_call | solution.py:303
  99.0 4.0 shard_map.287
  108.1 4.6 %collective-permute-done.15 = bf16[256,1536]{1,0:T(8,128)(2,1)S(1)} collective-permute-done((bf16[256,1536]{1,0:T(8,128)(2,1)S(1)}, bf16[256,1536]{1,0:T(8,128)(2,1)S(1)}, u32[]{:S(2)}, u32[]{:S(2)}) %collective-permute-start.15) | collective-permute-done | bytes 786464 | tf_op jit(solution)/shard_map/ppermute | solution.py:686
  112.8 8.4 %collective-permute-done.14 = bf16[256,1536]{1,0:T(8,128)(2,1)S(1)} collective-permute-done((bf16[256,1536]{1,0:T(8,128)(2,1)S(1)}, bf16[256,1536]{1,0:T(8,128)(2,1)S(1)}, u32[]{:S(2)}, u32[]{:S(2)}) %collective-permute-start.14) | collective-permute-done | bytes 786464 | tf_op jit(solution)/shard_map/ppermute | solution.py:58
  132.3 5.1 %collective-permute-done.17 = bf16[256,1536]{1,0:T(8,128)(2,1)} collective-permute-done((bf16[256,1536]{1,0:T(8,128)(2,1)}, bf16[256,1536]{1,0:T(8,128)(2,1)}, u32[]{:S(2)}, u32[]{:S(2)}) %collective-permute-start.17) | collective-permute-done | bytes 786464 | tf_op jit(solution)/shard_map/ppermute | solution.py:58
  173.8 11.4 %collective-permute-done.24.refs_4_ = bf16[256,1536]{1,0:T(8,128)(2,1)S(1)} collective-permute-done((bf16[256,1536]{1,0:T(8,128)(2,1)S(1)}, bf16[256,1536]{1,0:T(8,128)(2,1)S(1)}, u32[]{:S(2)}, u32[]{:S(2)}) %collective-permute-start.24) | collective-permute-done | bytes 786464 | tf_op jit(solution)/shard_map/ppermute | solution.py:58
  189.9 5.7 %shard_map.289 = (bf16[256,1536]{1,0:T(8,128)(2,1)S(1)}, bf16[264,1536]{1,0:T(8,128)(2,1)S(1)}, bf16[256,768]{1,0:T(8,128)(2,1)S(1)}, bf16[256,768]{1,0:T(8,128)...) custom-call(s32[1]{0:T(128)} %bitcast.2.refs_0_, ...), custom_call_target="tpu_custom_call" | custom-call | flops 3623878656 | tf_op jit(solution)/shard_map/pallas_call | solution.py:303
  195.7 7.2 %collective-permute-done.26.refs_4_ = bf16[256,1536]{1,0:T(8,128)(2,1)S(1)} collective-permute-done((bf16[256,1536]{1,0:T(8,128)(2,1)S(1)}, bf16[256,1536]{1,0:T(8,128)(2,1)S(1)}, u32[]{:S(2)}, u32[]{:S(2)}) %collective-permute-start.26) | collective-permute-done | bytes 786464 | tf_op jit(solution)/shard_map/ppermute | solution.py:58
  209.2 5.7 %shard_map.290 = (bf16[256,1536]{1,0:T(8,128)(2,1)S(1)}, bf16[264,1536]{1,0:T(8,128)(2,1)S(1)}, bf16[256,768]{1,0:T(8,128)(2,1)S(1)}, bf16[256,768]{1,0:T(8,128)...) custom-call(s32[1]{0:T(128)} %bitcast.2.refs_0_, ...), custom_call_target="tpu_custom_call" | custom-call | flops 3623878656 | tf_op jit(solution)/shard_map/pallas_call | solution.py:303
  215.1 6.2 %collective-permute-done.28.refs_4_ = bf16[256,1536]{1,0:T(8,128)(2,1)S(1)} collective-permute-done((bf16[256,1536]{1,0:T(8,128)(2,1)S(1)}, bf16[256,1536]{1,0:T(8,128)(2,1)S(1)}, u32[]{:S(2)}, u32[]{:S(2)}) %collective-permute-start.28) | collective-permute-done | bytes 786464 | tf_op jit(solution)/shard_map/ppermute | solution.py:58
  225.4 5.7 %shard_map.291 = (bf16[256,1536]{1,0:T(8,128)(2,1)S(1)}, bf16[264,1536]{1,0:T(8,128)(2,1)S(1)}, bf16[256,768]{1,0:T(8,128)(2,1)S(1)}, bf16[256,768]{1,0:T(8,128)...) custom-call(s32[1]{0:T(128)} %bitcast.2.refs_0_, ...), custom_call_target="tpu_custom_call" | custom-call | flops 3623878656 | tf_op jit(solution)/shard_map/pallas_call | solution.py:303
  240.9 7.4 %convolution_convert_fusion.2 = bf16[1536,768]{1,0:T(8,128)(2,1)S(1)} fusion(bf16[2048,1536]{1,0:T(8,128)(2,1)} %constant_dynamic-update-slice_fusion, bf16[2048,768]{1,0:T(8,128)(2,1)S(1)} %constant_dynamic-update-slice_fusion.8), kind=kOutput, calls=%fused_computation.3 | convolution fusion | flops 4833017856 | bytes 11796480 | tf_op jit(solution)/shard_map/dot_general | solution.py:28
  260.3 7.3 %convolution_convert_fusion.1 = bf16[1536,768]{1,0:T(8,128)(2,1)S(1)} fusion(bf16[2048,1536]{1,0:T(8,128)(2,1)S(1)} %bitcast.202, bf16[2048,768]{1,0:T(8,128)(2,1)} %constant_dynamic-update-slice_fusion.16), kind=kOutput, calls=%fused_computation.2 | convolution fusion | flops 4833017856 | bytes 11796480 | tf_op jit(solution)/shard_map/dot_general | solution.py:28
  277.0 7.3 %convolution_convert_fusion = bf16[768,1536]{1,0:T(8,128)(2,1)S(1)} fusion(bf16[2048,768]{1,0:T(8,128)(2,1)} %constant_dynamic-update-slice_fusion.24, bf16[2048,1536]{1,0:T(8,128)(2,1)S(1)} %constant_dynamic-update-slice_fusion.32), kind=kOutput, calls=%fused_computation.1 | convolution fusion | flops 4833017856 | bytes 11796480 | tf_op jit(solution)/shard_map/dot_general | solution.py:28
  284.7 3.9 collective-permute-done.37
  295.6 11.5 %collective-permute-done.42 = bf16[1,1,384,768]{3,2,1,0:T(8,128)(2,1)S(1)} collective-permute-done((bf16[1,1,384,768]{3,2,1,0:T(8,128)(2,1)S(1)}, bf16[1,1,384,768]{3,2,1,0:T(8,128)(2,1)S(1)}, u32[]{:S(2)}, u32[]{:S(2)}) %collective-permute-start.42) | collective-permute-done | bytes 589856 | tf_op jit(solution)/shard_map/ppermute | solution.py:135
  321.3 6.0 %shard_map.294.qkv = bf16[256,2048]{1,0:T(8,128)(2,1)S(1)} custom-call(bf16[256,1536]{1,0:T(8,128)(2,1)S(1)} %get-tuple-element.425.branch, bf16[3072,256]{1,0:T(8,128)(2,1)S(1)} %copy-done.12, bf16[256,1536]{1,0:T(8,128)(2,1)S(1)} %copy-done.15, bf16[256,256]{1,0:T(8,128)(2,1)S(1)} %copy-done.46, bf16[256,256]{1,0:T(8,128)(2,1)S(1)} %copy-done.47, ...), custom_call_target="tpu_custom_call" | custom-call | tf_op jit(solution)/shard_map/pallas_call | solution.py:303
  336.2 7.5 %collective-permute-done.44 = bf16[256,512]{1,0:T(8,128)(2,1)S(1)} collective-permute-done((bf16[256,512]{1,0:T(8,128)(2,1)S(1)}, bf16[256,512]{1,0:T(8,128)(2,1)S(1)}, u32[]{:S(2)}, u32[]{:S(2)}) %collective-permute-start.44) | collective-permute-done | bytes 262176 | tf_op jit(solution)/shard_map/ppermute | solution.py:704
  352.3 4.1 shard_map.295
  409.0 3.7 collective-permute-done.64
  (576 shorter events, 223.9 us)
Async XLA Ops:
  18.1 21.4 %collective-permute-start = (bf16[264,1536]{1,0:T(8,128)(2,1)}, bf16[264,1536]{1,0:T(8,128)(2,1)}, u32[]{:S(2)}, u32[]{:S(2)}) collective-permute-start(bf16[264,1536]{1,0:T(8,128)(2,1)} %get-tuple-element.245.refs_4_.refs_5_), channel_id=1, source_target_pairs={{0,2},{2,4},{4,6},{6,7},{7,5},{5,3},{3,1},{1,0},{8,10},{10,12},{12... | collective-permute-start | bytes 2433032 | tf_op jit(solution)/shard_map/ppermute | solution.py:58
  21.2 19.8 %collective-permute-start.1 = (bf16[264,1536]{1,0:T(8,128)(2,1)}, bf16[264,1536]{1,0:T(8,128)(2,1)}, u32[]{:S(2)}, u32[]{:S(2)}) collective-permute-start(bf16[264,1536]{1,0:T(8,128)(2,1)} %get-tuple-element.245.refs_4_.refs_5_), channel_id=1, source_target_pairs={{2,0},{4,2},{6,4},{7,6},{5,7},{3,5},{1,3},{0,1},{10,8},{12,10},{14... | collective-permute-start | bytes 2433032 | tf_op jit(solution)/shard_map/ppermute | solution.py:61
  41.0 19.9 %collective-permute-start.2 = (bf16[264,1536]{1,0:T(8,128)(2,1)}, bf16[264,1536]{1,0:T(8,128)(2,1)}, u32[]{:S(2)}, u32[]{:S(2)}) collective-permute-start(bf16[264,1536]{1,0:T(8,128)(2,1)} %collective-permute-done.refs_4_), channel_id=1, source_target_pairs={{0,2},{2,4},{4,6},{6,7},{7,5},{5,3},{3,1},{1,0},{8,10},{10,12},{12... | collective-permute-start | bytes 2433032 | tf_op jit(solution)/shard_map/ppermute | solution.py:58
  42.6 18.6 %collective-permute-start.3 = (bf16[264,1536]{1,0:T(8,128)(2,1)}, bf16[264,1536]{1,0:T(8,128)(2,1)}, u32[]{:S(2)}, u32[]{:S(2)}) collective-permute-start(bf16[264,1536]{1,0:T(8,128)(2,1)} %collective-permute-done.1.refs_5_), channel_id=1, source_target_pairs={{2,0},{4,2},{6,4},{7,6},{5,7},{3,5},{1,3},{0,1},{10,8},{12,10},{14... | collective-permute-start | bytes 2433032 | tf_op jit(solution)/shard_map/ppermute | solution.py:61
  43.0 17.8 %collective-permute-start.4 = (bf16[256,1536]{1,0:T(8,128)(2,1)}, bf16[256,1536]{1,0:T(8,128)(2,1)}, u32[]{:S(2)}, u32[]{:S(2)}) collective-permute-start(bf16[256,1536]{1,0:T(8,128)(2,1)} %get-tuple-element.430), channel_id=1, source_target_pairs={{0,16},{16,0},{1,17},{17,1},{2,18},{18,2},{3,19},{19,3},{4,20},{20... | collective-permute-start | bytes 2359304 | tf_op jit(solution)/shard_map/ppermute | solution.py:686
  62.8 18.3 %collective-permute-start.6 = (bf16[264,1536]{1,0:T(8,128)(2,1)}, bf16[264,1536]{1,0:T(8,128)(2,1)S(1)}, u32[]{:S(2)}, u32[]{:S(2)}) collective-permute-start(bf16[264,1536]{1,0:T(8,128)(2,1)} %collective-permute-done.3.refs_5_), channel_id=1, source_target_pairs={{2,0},{4,2},{6,4},{7,6},{5,7},{3,5},{1,3},{0,1},{10,8},{12,10},{14... | collective-permute-start | bytes 2433032 | tf_op jit(solution)/shard_map/ppermute | solution.py:61
  63.7 27.6 %collective-permute-start.10 = (bf16[256,1536]{1,0:T(8,128)(2,1)}, bf16[256,1536]{1,0:T(8,128)(2,1)S(1)}, u32[]{:S(2)}, u32[]{:S(2)}) collective-permute-start(bf16[256,1536]{1,0:T(8,128)(2,1)} %collective-permute-done.4), channel_id=1, source_target_pairs={{0,8},{8,0},{1,9},{9,1},{2,10},{10,2},{3,11},{11,3},{4,12},{12,4},... | collective-permute-start | bytes 2359304 | tf_op jit(solution)/shard_map/ppermute | solution.py:690
  63.7 27.6 %collective-permute-start.9 = (bf16[256,1536]{1,0:T(8,128)(2,1)S(1)}, bf16[256,1536]{1,0:T(8,128)(2,1)S(1)}, u32[]{:S(2)}, u32[]{:S(2)}) collective-permute-start(bf16[256,1536]{1,0:T(8,128)(2,1)S(1)} %copy-done.128), channel_id=1, source_target_pairs={{0,8},{8,0},{1,9},{9,1},{2,10},{10,2},{3,11},{11,3},{4,12},{12,4},... | collective-permute-start | bytes 2359304 | tf_op jit(solution)/shard_map/ppermute | solution.py:690
  131.7 33.0 %collective-permute-start.20 = (bf16[256,1536]{1,0:T(8,128)(2,1)}, bf16[256,1536]{1,0:T(8,128)(2,1)}, u32[]{:S(2)}, u32[]{:S(2)}) collective-permute-start(bf16[256,1536]{1,0:T(8,128)(2,1)} %get-tuple-element.434), channel_id=1, source_target_pairs={{0,8},{8,0},{1,9},{9,1},{2,10},{10,2},{3,11},{11,3},{4,12},{12,4},... | collective-permute-start | bytes 2359304 | tf_op jit(solution)/shard_map/ppermute | solution.py:690
  132.2 32.5 %collective-permute-start.21 = (bf16[256,1536]{1,0:T(8,128)(2,1)}, bf16[256,1536]{1,0:T(8,128)(2,1)}, u32[]{:S(2)}, u32[]{:S(2)}) collective-permute-start(bf16[256,1536]{1,0:T(8,128)(2,1)} %copy-done.136), channel_id=1, source_target_pairs={{0,8},{8,0},{1,9},{9,1},{2,10},{10,2},{3,11},{11,3},{4,12},{12,4},... | collective-permute-start | bytes 2359304 | tf_op jit(solution)/shard_map/ppermute | solution.py:690
  140.5 24.3 %collective-permute-start.19 = (bf16[256,1536]{1,0:T(8,128)(2,1)}, bf16[256,1536]{1,0:T(8,128)(2,1)}, u32[]{:S(2)}, u32[]{:S(2)}) collective-permute-start(bf16[256,1536]{1,0:T(8,128)(2,1)} %add_convert_fusion.7), channel_id=1, source_target_pairs={{0,2},{2,4},{4,6},{6,7},{7,5},{5,3},{3,1},{1,0},{8,10},{10,12},{12... | collective-permute-start | bytes 2359304 | tf_op jit(solution)/shard_map/ppermute | solution.py:58
  144.5 20.3 %collective-permute-start.18 = (bf16[256,1536]{1,0:T(8,128)(2,1)}, bf16[256,1536]{1,0:T(8,128)(2,1)}, u32[]{:S(2)}, u32[]{:S(2)}) collective-permute-start(bf16[256,1536]{1,0:T(8,128)(2,1)} %add_convert_fusion.8), channel_id=1, source_target_pairs={{2,0},{4,2},{6,4},{7,6},{5,7},{3,5},{1,3},{0,1},{10,8},{12,10},{14... | collective-permute-start | bytes 2359304 | tf_op jit(solution)/shard_map/ppermute | solution.py:61
  254.7 29.7 %collective-permute-start.38 = (bf16[2,1,384,768]{3,2,1,0:T(8,128)(2,1)S(1)}, bf16[2,1,384,768]{3,2,1,0:T(8,128)(2,1)S(1)}, u32[]{:S(2)}, u32[]{:S(2)}) collective-permute-start(bf16[2,1,384,768]{3,2,1,0:T(8,128)(2,1)S(1)} %constant_dynamic-slice_fusion.13), channel_id=1, source_target_pairs={{0,8},{8,0},{1,9},{9,1},{2,10},{10,2},{3,11},{11,3},{4,12},{12,4},... | collective-permute-start | bytes 3538952 | tf_op jit(solution)/shard_map/ppermute | solution.py:135
  268.1 20.5 %collective-permute-start.37 = (bf16[264,1536]{1,0:T(8,128)(2,1)S(1)}, bf16[264,1536]{1,0:T(8,128)(2,1)S(1)}, u32[]{:S(2)}, u32[]{:S(2)}) collective-permute-start(bf16[264,1536]{1,0:T(8,128)(2,1)S(1)} %add_convert_fusion.5), channel_id=1, source_target_pairs={{0,2},{2,4},{4,6},{6,7},{7,5},{5,3},{3,1},{1,0},{8,10},{10,12},{12... | collective-permute-start | bytes 2433032 | tf_op jit(solution)/shard_map/ppermute | solution.py:58
  268.7 20.2 %collective-permute-start.36 = (bf16[264,1536]{1,0:T(8,128)(2,1)S(1)}, bf16[264,1536]{1,0:T(8,128)(2,1)S(1)}, u32[]{:S(2)}, u32[]{:S(2)}) collective-permute-start(bf16[264,1536]{1,0:T(8,128)(2,1)S(1)} %add_convert_fusion.6), channel_id=1, source_target_pairs={{2,0},{4,2},{6,4},{7,6},{5,7},{3,5},{1,3},{0,1},{10,8},{12,10},{14... | collective-permute-start | bytes 2433032 | tf_op jit(solution)/shard_map/ppermute | solution.py:61
  271.1 24.2 %collective-permute-start.41 = (bf16[2,1,384,768]{3,2,1,0:T(8,128)(2,1)S(1)}, bf16[2,1,384,768]{3,2,1,0:T(8,128)(2,1)S(1)}, u32[]{:S(2)}, u32[]{:S(2)}) collective-permute-start(bf16[2,1,384,768]{3,2,1,0:T(8,128)(2,1)S(1)} %constant_dynamic-slice_fusion.12), channel_id=1, source_target_pairs={{0,8},{8,0},{1,9},{9,1},{2,10},{10,2},{3,11},{11,3},{4,12},{12,4},... | collective-permute-start | bytes 3538952 | tf_op jit(solution)/shard_map/ppermute | solution.py:135
  289.1 19.4 %collective-permute-start.40 = (bf16[264,1536]{1,0:T(8,128)(2,1)S(1)}, bf16[264,1536]{1,0:T(8,128)(2,1)S(1)}, u32[]{:S(2)}, u32[]{:S(2)}) collective-permute-start(bf16[264,1536]{1,0:T(8,128)(2,1)S(1)} %add_convert_fusion.3), channel_id=1, source_target_pairs={{0,2},{2,4},{4,6},{6,7},{7,5},{5,3},{3,1},{1,0},{8,10},{10,12},{12... | collective-permute-start | bytes 2433032 | tf_op jit(solution)/shard_map/ppermute | solution.py:58
  290.0 19.4 %collective-permute-start.39 = (bf16[264,1536]{1,0:T(8,128)(2,1)S(1)}, bf16[264,1536]{1,0:T(8,128)(2,1)S(1)}, u32[]{:S(2)}, u32[]{:S(2)}) collective-permute-start(bf16[264,1536]{1,0:T(8,128)(2,1)S(1)} %add_convert_fusion.4), channel_id=1, source_target_pairs={{2,0},{4,2},{6,4},{7,6},{5,7},{3,5},{1,3},{0,1},{10,8},{12,10},{14... | collective-permute-start | bytes 2433032 | tf_op jit(solution)/shard_map/ppermute | solution.py:61
  295.3 75.3 %collective-permute-start.77 = (bf16[2,1,192,1536]{3,2,1,0:T(8,128)(2,1)}, bf16[2,1,192,1536]{3,2,1,0:T(8,128)(2,1)}, u32[]{:S(2)}, u32[]{:S(2)}) collective-permute-start(bf16[2,1,192,1536]{3,2,1,0:T(8,128)(2,1)} %constant_dynamic-slice_fusion.1), channel_id=1, source_target_pairs={{0,8},{8,0},{1,9},{9,1},{2,10},{10,2},{3,11},{11,3},{4,12},{12,4},... | collective-permute-start | bytes 3538952 | tf_op jit(solution)/shard_map/ppermute | solution.py:135
  316.0 35.8 %collective-permute-start.49 = (bf16[1,1,384,768]{3,2,1,0:T(8,128)(2,1)}, bf16[1,1,384,768]{3,2,1,0:T(8,128)(2,1)}, u32[]{:S(2)}, u32[]{:S(2)}) collective-permute-start(bf16[1,1,384,768]{3,2,1,0:T(8,128)(2,1)} %constant_dynamic-slice_fusion.2), channel_id=1, source_target_pairs={{0,16},{16,0},{1,17},{17,1},{2,18},{18,2},{3,19},{19,3},{4,20},{20... | collective-permute-start | bytes 1769480 | tf_op jit(solution)/shard_map/ppermute | solution.py:135
  329.0 19.5 %collective-permute-start.45 = (bf16[256,512]{1,0:T(8,128)(2,1)S(1)}, bf16[256,512]{1,0:T(8,128)(2,1)S(1)}, u32[]{:S(2)}, u32[]{:S(2)}) collective-permute-start(bf16[256,512]{1,0:T(8,128)(2,1)S(1)} %get-tuple-element.490), channel_id=1, source_target_pairs={{0,24},{8,16},{16,8},{24,0},{1,25},{9,17},{17,9},{25,1},{2,26},{10... | collective-permute-start | bytes 786440 | tf_op jit(solution)/shard_map/ppermute | solution.py:704
  334.7 29.0 %collective-permute-start.66 = (bf16[96,384]{1,0:T(8,128)(2,1)}, bf16[96,384]{1,0:T(8,128)(2,1)}, u32[]{:S(2)}, u32[]{:S(2)}) collective-permute-start(bf16[96,384]{1,0:T(8,128)(2,1)} %get-tuple-element.484), channel_id=1, source_target_pairs={{2,0},{4,2},{6,4},{7,6},{5,7},{3,5},{1,3},{0,1},{10,8},{12,10},{14... | collective-permute-start | bytes 221192 | tf_op jit(solution)/shard_map/ppermute | solution.py:61
  343.7 20.2 %collective-permute-start.67 = (bf16[96,384]{1,0:T(8,128)(2,1)}, bf16[96,384]{1,0:T(8,128)(2,1)}, u32[]{:S(2)}, u32[]{:S(2)}) collective-permute-start(bf16[96,384]{1,0:T(8,128)(2,1)} %get-tuple-element.485), channel_id=1, source_target_pairs={{0,2},{2,4},{4,6},{6,7},{7,5},{5,3},{3,1},{1,0},{8,10},{10,12},{12... | collective-permute-start | bytes 221192 | tf_op jit(solution)/shard_map/ppermute | solution.py:58
  381.9 25.7 %collective-permute-start.78 = (bf16[1,1,192,1536]{3,2,1,0:T(8,128)(2,1)}, bf16[1,1,192,1536]{3,2,1,0:T(8,128)(2,1)S(1)}, u32[]{:S(2)}, u32[]{:S(2)}) collective-permute-start(bf16[1,1,192,1536]{3,2,1,0:T(8,128)(2,1)} %constant_dynamic-slice_fusion), channel_id=1, source_target_pairs={{0,16},{16,0},{1,17},{17,1},{2,18},{18,2},{3,19},{19,3},{4,20},{20... | collective-permute-start | bytes 1769480 | tf_op jit(solution)/shard_map/ppermute | solution.py:135
  (197 other events, 1656.1 us)
